TPU v7x, 32 devices: a whole 2x2x4 slice. The times are simulated.
32 devices in a mesh: groups: 2 (over y), dp: 4 (over x, core), tensor: 4 (over z).
Axes of the slice: x: 2, y: 2, z: 4, core: 2. Of those that a mesh axis runs over, the one named last changes fastest.
Arguments:
- hidden: bfloat16 [8192, 8192], P(('groups', 'dp'), 'tensor'), parts along dimension 0, may hold values from -6 to 6
- key_value_weight: bfloat16 [8192, 2048], P('tensor'), may hold values from -0.0625 to 0.0625
- adapter_down_factors: bfloat16 [8192, 512], P('tensor', 'dp'), may hold values from -0.0625 to 0.0625
- adapter_up_factors: bfloat16 [512, 2048], P('dp', 'tensor'), may hold values from -0.75 to 0.75
- row_adapter: int32 [8192, 1], P(('groups', 'dp')), parts along dimension 0, may hold values from 0 to 7; in each aligned block of 1024 rows (0 to 1023, 1024 to 2047, ...) at most 256 rows name the same one
- rank_of_adapter: int32 [8], replicated, may hold values from 16 to 64
- adapter_storage_slot: int32 [8], replicated, may hold values from 0 to 7, each once
Outputs:
- projected: bfloat16 [8192, 2048], P(('groups', 'dp'), 'tensor'), parts along dimension 0
There are 2 independent parts, one for each index of `groups`. A program takes and returns all parts, laid end to end along the dimension named above; an argument that names none is the same for every part. Nothing has to cross between parts.
Inputs may be any that keep to these rules, and one draw needn't show every extreme that they name: `row_adapter`: in the rows of one index of dp no adapter is named more than 256 times, a bound that some block reaches. `adapter_storage_slot`: each slot holds one adapter.
All inputs are finite; a program needn't handle non-finite values.
Results may differ from a plain program's by a relative error of at most 0.013.
Values may be sent and summed in bfloat16 or wider, within the bound.
No kernel may reach another device: no remote copies, remote signals or barrier semaphores. Data moves between devices by JAX's collectives and lax.ppermute only.
A program may use at most 128 MiB of HBM per device.

v0:
```python
import jax
import jax.numpy as jnp
from jax import lax
from jax.sharding import PartitionSpec as P


def on_device(
    hidden,
    key_value_weight,
    adapter_down_factors,
    adapter_up_factors,
    row_adapter,
    rank_of_adapter,
    adapter_storage_slot,
):
    row_count = hidden.shape[0]
    adapter_table = rank_of_adapter.shape[0]
    rank_width = (
        adapter_up_factors.shape[0]
        // adapter_up_factors.shape[0]
        * (adapter_down_factors.shape[1] * lax.axis_size("dp") // adapter_table)
    )
    row_ids = row_adapter[:, 0]
    every_id = jnp.arange(adapter_table, dtype=jnp.int32)
    id_match = row_ids[:, None] == every_id[None, :]
    slot_row = jnp.sum(jnp.where(id_match, adapter_storage_slot[None, :], 0), axis=1)
    rank_row = jnp.sum(jnp.where(id_match, rank_of_adapter[None, :], 0), axis=1)
    slot_match = slot_row[:, None] == every_id[None, :]
    partial_sum = jnp.dot(hidden, key_value_weight, preferred_element_type=jnp.float32)
    base_sum = lax.psum_scatter(
        partial_sum.astype(jnp.bfloat16), "tensor", scatter_dimension=1, tiled=True
    ).astype(jnp.float32)
    block_columns = lax.all_gather(adapter_down_factors, "dp", axis=1, tiled=True)
    count = block_columns.shape[1] // rank_width
    product = jnp.dot(hidden, block_columns, preferred_element_type=jnp.float32)
    chosen = slot_match.astype(jnp.float32)
    low_part = jnp.einsum("rac,ra->rc", product.reshape(row_count, count, rank_width), chosen)
    low_full = lax.psum(low_part.astype(jnp.bfloat16), "tensor").astype(jnp.float32)
    columns = jnp.arange(rank_width, dtype=jnp.int32)
    live_cols = columns[None, :] < rank_row[:, None]
    scaling = rank_width / (2.0 * rank_row.astype(jnp.float32))
    low_rank = jnp.where(live_cols, low_full * scaling[:, None], jnp.float32(0.0)).astype(
        jnp.bfloat16
    )
    spread = jnp.where(slot_match[:, :, None], low_rank[:, None, :], jnp.zeros((), jnp.bfloat16))
    spread = spread.reshape(row_count, adapter_table * rank_width)
    up_factor_rows = lax.all_gather(adapter_up_factors, "dp", axis=0, tiled=True)
    adapter_out = jnp.dot(spread, up_factor_rows, preferred_element_type=jnp.float32)
    return (base_sum + adapter_out).astype(jnp.bfloat16)


def solution(mesh):
    placed = (
        P(("groups", "dp"), "tensor"),
        P("tensor", None),
        P("tensor", "dp"),
        P("dp", "tensor"),
        P(("groups", "dp"), None),
        P(),
        P(),
    )
    return jax.shard_map(
        on_device,
        mesh=mesh,
        in_specs=placed,
        out_specs=P(("groups", "dp"), "tensor"),
        check_vma=False,
    )
```

profile of v0, /device:TPU:0, one launch (start us, length us, event | category | flops | bytes accessed | tf_op | source)
XLA Modules:
  0.0 163.5 jit_solution(15673058449753426550)
XLA Ops:
  6.5 0.0 all-gather.2.cloned.1.call-start
  6.5 0.7 all-gather.2.cloned.1.call-update
  7.3 0.0 all-reduce.2.cloned.1.call-start
  7.3 0.8 select_reduce_fusion
  8.1 26.4 %all-gather.2.cloned.1.call-done = bf16[2048,512]{1,0:T(8,128)(2,1)} async-done(((bf16[2048,128]{1,0:T(8,128)(2,1)}), bf16[2048,512]{1,0:T(8,128)(2,1)}) %all-gather.2.cloned.1.call-update) | async-done | bytes 2097168 | tf_op jit(solution)/shard_map/all_gather | solution.py:33
  34.5 5.2 %fusion.1 = f32[1024,512]{0,1:T(8,128)S(1)} fusion(bf16[1024,2048]{1,0:T(8,128)(2,1)} %param.7, bf16[2048,512]{1,0:T(8,128)(2,1)} %all-gather.2.cloned.1.call-done), kind=kOutput, calls=%fused_computation.12 | convolution fusion | flops 2147483648 | bytes 8388608 | tf_op jit(solution)/shard_map/dot_general | solution.py:35
  39.7 0.9 multiply_reduce_fusion
  40.6 0.0 all-reduce.2.cloned.1.call-update
  40.6 0.0 reduce-scatter.2.cloned.1.call-start
  40.7 13.8 %convolution_convert_fusion = bf16[1024,2048]{1,0:T(8,128)(2,1)} fusion(bf16[1024,2048]{1,0:T(8,128)(2,1)} %param.7, bf16[2048,2048]{1,0:T(8,128)(2,1)} %param.8), kind=kOutput, calls=%fused_computation | convolution fusion | flops 8592031744 | bytes 16777216 | tf_op jit(solution)/shard_map/dot_general | solution.py:29
  54.5 0.0 copy-start
  54.5 0.0 reduce-scatter.2.cloned.1.call-update
  54.5 0.9 copy-done
  55.4 7.2 %all_gather.7 = bf16[512,512]{1,0:T(8,128)(2,1)S(1)} all-gather(bf16[128,512]{1,0:T(8,128)(2,1)S(1)} %copy-done), channel_id=1, replica_groups=mesh['groups'=2,'dp'=4,'tensor'=4] {'dp'}, dimensions={0}, use_global_device_ids=true | all-gather | bytes 655360 | tf_op jit(solution)/shard_map/all_gather | solution.py:47
  62.6 12.6 %all-reduce.2.cloned.1.call-done = bf16[1024,64]{0,1:T(8,128)(2,1)} async-done(((bf16[1024,64]{0,1:T(8,128)(2,1)}), bf16[1024,64]{0,1:T(8,128)(2,1)}) %all-reduce.2.cloned.1.call-update) | async-done | bytes 131088 | tf_op jit(solution)/shard_map/psum | solution.py:38
  75.2 0.9 select_convert_fusion
  76.2 0.1 broadcast_select_fusion
  76.3 77.8 %reduce-scatter.2.cloned.1.call-done = bf16[1024,512]{1,0:T(8,128)(2,1)} async-done(((bf16[1024,2048]{1,0:T(8,128)(2,1)}), bf16[1024,512]{1,0:T(8,128)(2,1)}) %reduce-scatter.2.cloned.1.call-update) | async-done | bytes 1048592 | tf_op jit(solution)/shard_map/reduce_scatter | solution.py:30
  154.1 2.9 %add_convert_fusion = bf16[1024,512]{1,0:T(8,128)(2,1)} fusion(bf16[1024,512]{1,0:T(8,128)(2,1)} %reduce-scatter.2.cloned.1.call-done, bf16[1024,512]{0,1:T(8,128)(2,1)S(1)} %bitcast.10, bf16[512,512]{1,0:T(8,128)(2,1)S(1)} %all_gather.7), kind=kOutput, calls=%fused_computation.2 | convolution fusion | flops 538443776 | bytes 3670016 | tf_op jit(solution)/shard_map/dot_general | solution.py:48
  (2 shorter events, 0.0 us)
Async XLA Ops:
  6.5 27.9 %all-gather.2.cloned.1.call-start = ((), (), s32[]{:S(2)}) async-start(), calls=%async_computation.2 | async-start | bytes 2621440 | tf_op jit(solution)/shard_map/all_gather | solution.py:33
  7.3 68.0 %all-reduce.2.cloned.1.call-start = ((), (), s32[]{:S(2)}) async-start(), calls=%async_computation.3 | async-start | bytes 262144 | tf_op jit(solution)/shard_map/psum | solution.py:38
  40.6 113.4 %reduce-scatter.2.cloned.1.call-start = ((), (), s32[]{:S(2)}) async-start(), calls=%async_computation.1 | async-start | bytes 5242880 | tf_op jit(solution)/shard_map/reduce_scatter | solution.py:30
  54.5 0.9 copy-start
Sparse Core Ops, SparseCore 0:
  8.9 25.5 all-gather.1
  40.8 34.4 all-reduce.1
  77.6 76.3 reduce-scatter.1
where the time goes:
time: 164 us
  waiting for transfers between devices  118 us (72%)
  matrix products  22 us (13%)
  between operations  13.1 us (8%)
  blocking collectives  7.19 us (4%)
  other arithmetic  2.72 us (2%)
    reduce_scatter x1, waiting for transfers between devices, on_device(): lax.psum_scatter(partial_sum.astype(jnp.bfloat16), 'tensor', scatter_dime...  77.8 us
    all_gather x1, waiting for transfers between devices, on_device(): lax.all_gather(adapter_down_factors, 'dp', axis=1, tiled=True)  26.4 us
    dot_general x1, matrix products, on_device(): jnp.dot(hidden, key_value_weight, preferred_element_type=jnp.float32)  13.8 us
    psum x1, waiting for transfers between devices, on_device(): lax.psum(low_part.astype(jnp.bfloat16), 'tensor').astype(jnp.float32)  12.6 us
    all_gather x1, blocking collectives, on_device(): lax.all_gather(adapter_up_factors, 'dp', axis=0, tiled=True)  7.19 us
    dot_general x1, matrix products, on_device(): product = jnp.dot(hidden, block_columns, preferred_element_type=jnp.float32)  5.23 us
  transfers between devices with their start and end apart: 3, of which 3 were waited for; matrix products, arithmetic and copies ran while one was open for 10% of the time, Pallas kernels for 0%

commit v1 on v0

v1 whole, which is shorter than its diff:
```python
import jax
import jax.numpy as jnp
from jax import lax
from jax.sharding import PartitionSpec as P

F32 = jnp.float32
BF16 = jnp.bfloat16


def gather_dp(block, axis, size):
    held = block
    bit = size // 2
    while bit:
        other = lax.ppermute(held, "dp", [(i, i ^ bit) for i in range(size)])
        held = (held, other, bit)
        bit //= 2
    return held


def line_of_four(
    hidden, weight, down, up, row_adapter, rank_of_adapter, adapter_storage_slot
):
    rows = hidden.shape[0]
    half = rows // 2
    cols = weight.shape[1] // 4
    dp = lax.axis_size("dp")
    adapters = rank_of_adapter.shape[0]
    width = down.shape[1] * dp // adapters
    per_dev = adapters // dp
    me = lax.axis_index("tensor")
    at = lax.axis_index("dp")

    table = jnp.array([[3, 2, 1, 0], [3, 2, 0, 1], [0, 1, 3, 2], [0, 1, 2, 3]], jnp.int32)

    def part(phase, lo, hi):
        block = lax.dynamic_slice_in_dim(weight, table[me, phase] * cols, cols, 1)
        return jnp.dot(hidden[lo:hi], block, preferred_element_type=F32)

    ends = [(0, 1), (3, 2)]
    middle = [(1, 2), (2, 1)]
    outward = [(2, 3), (1, 0)]

    def send(v, pairs):
        return lax.ppermute(v, "tensor", pairs)

    def add(a, b):
        return (a.astype(F32) + b.astype(F32)).astype(BF16)

    spans = [(0, half), (half, rows)]
    p0 = [part(0, *s).astype(BF16) for s in spans]
    a1 = [send(v, ends) for v in p0]

    def gather(block, axis):
        bit = dp // 2
        while bit:
            other = lax.ppermute(block, "dp", [(i, i ^ bit) for i in range(dp)])
            block = (block, other)
            block = jnp.concatenate(block, axis)
            bit //= 2
        return block

    place = [0]
    bit = dp // 2
    while bit:
        place = place + [p ^ bit for p in place]
        bit //= 2
    owner_at = jnp.array(place, jnp.int32) ^ at

    downs = gather(down, 1)
    ups = gather(up, 0)

    p1 = [part(1, *s).astype(BF16) for s in spans]
    a2 = [send(v, ends) for v in p1]
    b1 = [send(add(p, a), middle) for p, a in zip(p0, a1)]

    ids = row_adapter[:, 0]
    match = ids[:, None] == jnp.arange(adapters, dtype=jnp.int32)[None, :]
    slot = jnp.sum(jnp.where(match, adapter_storage_slot[None, :], 0), axis=1)
    rank = jnp.sum(jnp.where(match, rank_of_adapter[None, :], 0), axis=1)
    slot_at = (owner_at[:, None] * per_dev + jnp.arange(per_dev, dtype=jnp.int32)[None, :]).reshape(-1)
    chosen = slot[:, None] == slot_at[None, :]
    product = jnp.dot(hidden, downs, preferred_element_type=F32)
    low = jnp.einsum("rac,ra->rc", product.reshape(rows, adapters, width), chosen.astype(F32)).astype(BF16)
    e1 = send(low, ends)
    low = add(low, e1)
    e2 = send(low, middle)
    low = add(low, e2)
    e3 = send(low, outward)
    is_end = (me == 0) | (me == 3)
    low = jnp.where(is_end, e3, low).astype(F32)

    p2 = [part(2, *s).astype(BF16) for s in spans]
    a3 = [send(v, ends) for v in p2]
    b2 = [send(add(p, a), middle) for p, a in zip(p1, a2)]
    d1 = [send(add(p, a), outward) for p, a in zip(p2, b1)]

    live = jnp.arange(width, dtype=jnp.int32)[None, :] < rank[:, None]
    scaling = width / (2.0 * rank.astype(F32))
    low_rank = jnp.where(live, low * scaling[:, None], F32(0.0)).astype(BF16)
    spread = jnp.where(chosen[:, :, None], low_rank[:, None, :], jnp.zeros((), BF16)).reshape(rows, -1)
    out = []
    for k, s in enumerate(spans):
        own = part(3, *s) + jnp.dot(spread[s[0] : s[1]], ups, preferred_element_type=F32)
        total = own + b2[k].astype(F32) + d1[k].astype(F32)
        out.append((total + a3[k].astype(F32)).astype(BF16))
    return jnp.concatenate(out, 0)


def any_line(
    hidden, weight, down, up, row_adapter, rank_of_adapter, adapter_storage_slot
):
    rows = hidden.shape[0]
    adapters = rank_of_adapter.shape[0]
    width = down.shape[1] * lax.axis_size("dp") // adapters
    ids = row_adapter[:, 0]
    every = jnp.arange(adapters, dtype=jnp.int32)
    match = ids[:, None] == every[None, :]
    slot = jnp.sum(jnp.where(match, adapter_storage_slot[None, :], 0), axis=1)
    rank = jnp.sum(jnp.where(match, rank_of_adapter[None, :], 0), axis=1)
    chosen = slot[:, None] == every[None, :]
    partial = jnp.dot(hidden, weight, preferred_element_type=F32).astype(BF16)
    base = lax.psum_scatter(partial, "tensor", scatter_dimension=1, tiled=True).astype(F32)
    downs = lax.all_gather(down, "dp", axis=1, tiled=True)
    product = jnp.dot(hidden, downs, preferred_element_type=F32)
    low = jnp.einsum("rac,ra->rc", product.reshape(rows, adapters, width), chosen.astype(F32))
    low = lax.psum(low.astype(BF16), "tensor").astype(F32)
    live = jnp.arange(width, dtype=jnp.int32)[None, :] < rank[:, None]
    scaling = width / (2.0 * rank.astype(F32))
    low_rank = jnp.where(live, low * scaling[:, None], F32(0.0)).astype(BF16)
    spread = jnp.where(chosen[:, :, None], low_rank[:, None, :], jnp.zeros((), BF16)).reshape(rows, -1)
    ups = lax.all_gather(up, "dp", axis=0, tiled=True)
    return (base + jnp.dot(spread, ups, preferred_element_type=F32)).astype(BF16)


def solution(mesh):
    four = mesh.shape["tensor"] == 4 and mesh.shape["dp"] & (mesh.shape["dp"] - 1) == 0
    return jax.shard_map(
        line_of_four if four else any_line,
        mesh=mesh,
        in_specs=(
            P(("groups", "dp"), "tensor"),
            P("tensor", None),
            P("tensor", "dp"),
            P("dp", "tensor"),
            P(("groups", "dp"), None),
            P(),
            P(),
        ),
        out_specs=P(("groups", "dp"), "tensor"),
        check_vma=False,
    )
```

time: 164 us -> 149 us (0.909)
  waiting for transfers between devices: 118 us -> 71.1 us
  starting transfers between devices: 0.08 us -> 29.3 us
  matrix products: 22 us -> 35.4 us
  between operations: 13.1 us -> 3 us
  blocking collectives: 7.19 us -> 0 us
  other arithmetic: 2.72 us -> 6.86 us
  local copies, waits for them, and re-layouts: 0.88 us -> 2.75 us
    reduce_scatter x1 -> x0, waiting for transfers between devices: 77.8 us -> none  [on_device(): lax.psum_scatter(partial_sum.astype(jnp.bfloat16), 'tensor', scatter_dime...]
    ppermute x0 -> x19, waiting for transfers between devices: none -> 71.1 us  [the longest x15 71 us: send(): return lax.ppermute(v, 'tensor', pairs)]
    ppermute x0 -> x19, starting transfers between devices: none -> 29.3 us  [the longest x15 25.7 us: send(): return lax.ppermute(v, 'tensor', pairs)]
    all_gather x1 -> x0, waiting for transfers between devices: 26.4 us -> none  [on_device(): lax.all_gather(adapter_down_factors, 'dp', axis=1, tiled=True)]
    dot_general x3 -> x11, matrix products: 22 us -> 35.4 us  [the longest x8 28 us: part(): return jnp.dot(hidden[lo:hi], block, preferred_element_type=F32)]
    psum x1 -> x0, waiting for transfers between devices: 12.6 us -> none  [on_device(): lax.psum(low_part.astype(jnp.bfloat16), 'tensor').astype(jnp.float32)]
    all_gather x1 -> x0, blocking collectives: 7.19 us -> none  [on_device(): lax.all_gather(adapter_up_factors, 'dp', axis=0, tiled=True)]
    concatenate x0 -> x3, other arithmetic: none -> 2.93 us  [the longest x2 1.89 us: gather(): block = jnp.concatenate(block, axis)]
  transfers between devices with their start and end apart: 3 -> 19, of which waited for: 3 -> 7; matrix products, arithmetic and copies ran while one was open for 10% -> 29% of each run, Pallas kernels for 0% -> 0%
where the time goes in v1:
time: 149 us; the launch traced here: 148 us
  waiting for transfers between devices  71.1 us (48%)
  matrix products  35.4 us (24%)
  starting transfers between devices  29.3 us (20%)
  other arithmetic  6.86 us (5%)
  between operations  3 us (2%)
  local copies, waits for them, and re-layouts  2.75 us (2%)
    ppermute x15, waiting for transfers between devices, send(): return lax.ppermute(v, 'tensor', pairs)  71 us
    dot_general x8, matrix products, part(): return jnp.dot(hidden[lo:hi], block, preferred_element_type=F32)  28 us
    ppermute x15, starting transfers between devices, send(): return lax.ppermute(v, 'tensor', pairs)  25.7 us
    dot_general x1, matrix products, line_of_four(): product = jnp.dot(hidden, downs, preferred_element_type=F32)  5.07 us
    ppermute x4, starting transfers between devices, gather(): other = lax.ppermute(block, 'dp', [(i, i ^ bit) for i in range(dp)])  3.54 us
    convert_element_type x8, other arithmetic, add(): return (a.astype(F32) + b.astype(F32)).astype(BF16)  3.29 us
  transfers between devices with their start and end apart: 19, of which 7 were waited for; matrix products, arithmetic and copies ran while one was open for 29% of the time, Pallas kernels for 0%

profile of v1, /device:TPU:0, one launch (start us, length us, event | category | flops | bytes accessed | tf_op | source)
XLA Modules:
  0.0 148.4 jit_solution(6731267240483440486)
XLA Ops:
  0.0 2.9 %collective-permute-start = (bf16[2048,128]{1,0:T(8,128)(2,1)}, bf16[2048,128]{1,0:T(8,128)(2,1)}, u32[]{:S(2)}, u32[]{:S(2)}) collective-permute-start(bf16[2048,128]{1,0:T(8,128)(2,1)} %param.11), channel_id=1, source_target_pairs={{0,8},{4,12},{8,0},{12,4},{1,9},{5,13},{9,1},{13,5},{2,10},{6,14},... | collective-permute-start | bytes 1572872 | tf_op jit(solution)/shard_map/ppermute | solution.py:56
  3.0 1.5 %constant_dynamic-slice_fusion.1 = (s32[1,1]{1,0:T(1,128)}, s32[1,1]{1,0:T(1,128)}, s32[1,1]{1,0:T(1,128)}, s32[1,1]{1,0:T(1,128)}) fusion(s32[4,4]{1,0:T(4,128)} %constant.38.clone, s32[]{:T(128)S(6)} %select_n.49), kind=kLoop, calls=%fused_computation.87 | loop fusion | bytes 36 | tf_op jit(solution)/shard_map/dynamic_slice | solution.py:36
  5.0 3.5 %fusion.89 = bf16[512,512]{1,0:T(8,128)(2,1)S(1)} fusion(bf16[2048,2048]{1,0:T(8,128)(2,1)} %param.10, s32[]{:T(128)S(6)} %select_n.58, bf16[1024,2048]{1,0:T(8,128)(2,1)} %param.9), kind=kOutput, calls=%fused_computation.52 | convolution fusion | flops 1074003968 | bytes 4718596 | tf_op jit(solution)/shard_map/dot_general | solution.py:37
  8.5 4.9 %collective-permute-start.18 = (bf16[512,512]{1,0:T(8,128)(2,1)S(1)}, bf16[512,512]{1,0:T(8,128)(2,1)}, u32[]{:S(2)}, u32[]{:S(2)}) collective-permute-start(bf16[512,512]{1,0:T(8,128)(2,1)S(1)} %fusion.89), channel_id=1, source_target_pairs={{0,1},{3,2},{4,5},{7,6},{8,9},{11,10},{12,13},{15,14},{16,17},{19,... | collective-permute-start | bytes 1572872 | tf_op jit(solution)/shard_map/ppermute | solution.py:44
  14.0 4.3 %fusion.79 = bf16[512,512]{1,0:T(8,128)(2,1)} fusion(bf16[2048,2048]{1,0:T(8,128)(2,1)} %param.10, s32[]{:T(128)S(6)} %select_n.59, bf16[1024,2048]{1,0:T(8,128)(2,1)} %param.9), kind=kOutput, calls=%fused_computation.50 | convolution fusion | flops 1074003968 | bytes 4718596 | tf_op jit(solution)/shard_map/dot_general | solution.py:37
  18.3 2.1 %collective-permute-start.15 = (bf16[512,512]{1,0:T(8,128)(2,1)}, bf16[512,512]{1,0:T(8,128)(2,1)}, u32[]{:S(2)}, u32[]{:S(2)}) collective-permute-start(bf16[512,512]{1,0:T(8,128)(2,1)} %fusion.79), channel_id=1, source_target_pairs={{0,1},{3,2},{4,5},{7,6},{8,9},{11,10},{12,13},{15,14},{16,17},{19,... | collective-permute-start | bytes 1572872 | tf_op jit(solution)/shard_map/ppermute | solution.py:44
  21.1 4.3 %fusion.99 = bf16[512,512]{1,0:T(8,128)(2,1)} fusion(bf16[2048,2048]{1,0:T(8,128)(2,1)} %param.10, s32[]{:T(128)S(6)} %select_n.57, bf16[1024,2048]{1,0:T(8,128)(2,1)} %param.9), kind=kOutput, calls=%fused_computation.54 | convolution fusion | flops 1074003968 | bytes 4718596 | tf_op jit(solution)/shard_map/dot_general | solution.py:37
  25.3 2.1 %collective-permute-start.13 = (bf16[512,512]{1,0:T(8,128)(2,1)}, bf16[512,512]{1,0:T(8,128)(2,1)}, u32[]{:S(2)}, u32[]{:S(2)}) collective-permute-start(bf16[512,512]{1,0:T(8,128)(2,1)} %fusion.99), channel_id=1, source_target_pairs={{0,1},{3,2},{4,5},{7,6},{8,9},{11,10},{12,13},{15,14},{16,17},{19,... | collective-permute-start | bytes 1572872 | tf_op jit(solution)/shard_map/ppermute | solution.py:44
  28.2 4.6 %fusion.22 = f32[512,512]{1,0:T(8,128)} fusion(bf16[2048,2048]{1,0:T(8,128)(2,1)} %param.10, s32[]{:T(128)S(6)} %select_n.50, bf16[1024,2048]{1,0:T(8,128)(2,1)} %param.9), kind=kOutput, calls=%fused_computation.23 | convolution fusion | flops 1073741824 | bytes 5242884 | tf_op jit(solution)/shard_map/dot_general | solution.py:37
  32.8 3.6 %fusion.25 = f32[512,512]{1,0:T(8,128)S(1)} fusion(bf16[2048,2048]{1,0:T(8,128)(2,1)} %param.10, s32[]{:T(128)S(6)} %select_n.50, bf16[1024,2048]{1,0:T(8,128)(2,1)} %param.9), kind=kOutput, calls=%fused_computation.24 | convolution fusion | flops 1073741824 | bytes 5242884 | tf_op jit(solution)/shard_map/dot_general | solution.py:37
  36.4 3.7 %fusion.84 = bf16[512,512]{1,0:T(8,128)(2,1)} fusion(bf16[2048,2048]{1,0:T(8,128)(2,1)} %param.10, s32[]{:T(128)S(6)} %select_n.58, bf16[1024,2048]{1,0:T(8,128)(2,1)S(1)} %copy-done.10), kind=kOutput, calls=%fused_computation.51 | convolution fusion | flops 1074003968 | bytes 4718596 | tf_op jit(solution)/shard_map/dot_general | solution.py:37
  40.1 2.1 %fusion.74 = bf16[512,512]{1,0:T(8,128)(2,1)} fusion(bf16[2048,2048]{1,0:T(8,128)(2,1)S(1)} %bitcast.36, s32[]{:T(128)S(6)} %select_n.59, bf16[1024,2048]{1,0:T(8,128)(2,1)S(1)} %copy-done.10), kind=kOutput, calls=%fused_computation.49 | convolution fusion | flops 1074003968 | bytes 4718596 | tf_op jit(solution)/shard_map/dot_general | solution.py:37
  42.2 2.1 %fusion.94 = bf16[512,512]{1,0:T(8,128)(2,1)} fusion(bf16[2048,2048]{1,0:T(8,128)(2,1)S(1)} %bitcast.36, s32[]{:T(128)S(6)} %select_n.57, bf16[1024,2048]{1,0:T(8,128)(2,1)S(1)} %copy-done.10), kind=kOutput, calls=%fused_computation.53 | convolution fusion | flops 1074003968 | bytes 4718596 | tf_op jit(solution)/shard_map/dot_general | solution.py:37
  47.2 1.4 collective-permute-start.12
  49.7 1.5 collective-permute-start.9
  55.2 17.3 %collective-permute-done.9 = bf16[512,512]{1,0:T(8,128)(2,1)S(1)} collective-permute-done((bf16[512,512]{1,0:T(8,128)(2,1)}, bf16[512,512]{1,0:T(8,128)(2,1)S(1)}, u32[]{:S(2)}, u32[]{:S(2)}) %collective-permute-start.9) | collective-permute-done | bytes 524320 | tf_op jit(solution)/shard_map/ppermute | solution.py:44
  74.0 5.1 %fusion = f32[512,1024]{1,0:T(8,128)S(1)} fusion(bf16[1024,2048]{1,0:T(8,128)(2,1)} %param.9, bf16[2048,256]{1,0:T(8,128)(2,1)} %collective-permute-done.1, bf16[2048,128]{1,0:T(8,128)(2,1)} %collective-permute-done, bf16[2048,128]{1,0:T(8,128)(2,1)S(1)} %copy-done.6), kind=kOutput, calls=%fused_computation | convolution fusion | flops 2153775104 | bytes 8388608 | tf_op jit(solution)/shard_map/dot_general | solution.py:82
  79.3 3.7 %collective-permute-done.7 = bf16[512,512]{1,0:T(8,128)(2,1)S(1)} collective-permute-done((bf16[512,512]{1,0:T(8,128)(2,1)S(1)}, bf16[512,512]{1,0:T(8,128)(2,1)S(1)}, u32[]{:S(2)}, u32[]{:S(2)}) %collective-permute-start.7) | collective-permute-done | bytes 524320 | tf_op jit(solution)/shard_map/ppermute | solution.py:44
  83.1 5.1 %collective-permute-start.2 = (bf16[1024,64]{0,1:T(8,128)(2,1)S(1)}, bf16[1024,64]{0,1:T(8,128)(2,1)S(1)}, u32[]{:S(2)}, u32[]{:S(2)}) collective-permute-start(bf16[1024,64]{0,1:T(8,128)(2,1)S(1)} %multiply_reduce_fusion), channel_id=1, source_target_pairs={{0,1},{3,2},{4,5},{7,6},{8,9},{11,10},{12,13},{15,14},{16,17},{19,... | collective-permute-start | bytes 393224 | tf_op jit(solution)/shard_map/ppermute | solution.py:44
  88.4 2.4 %collective-permute-done.2 = bf16[1024,64]{0,1:T(8,128)(2,1)S(1)} collective-permute-done((bf16[1024,64]{0,1:T(8,128)(2,1)S(1)}, bf16[1024,64]{0,1:T(8,128)(2,1)S(1)}, u32[]{:S(2)}, u32[]{:S(2)}) %collective-permute-start.2) | collective-permute-done | bytes 131104 | tf_op jit(solution)/shard_map/ppermute | solution.py:44
  94.5 28.2 %collective-permute-done.4 = bf16[1024,64]{0,1:T(8,128)(2,1)S(1)} collective-permute-done((bf16[1024,64]{0,1:T(8,128)(2,1)S(1)}, bf16[1024,64]{0,1:T(8,128)(2,1)S(1)}, u32[]{:S(2)}, u32[]{:S(2)}) %collective-permute-start.4) | collective-permute-done | bytes 131104 | tf_op jit(solution)/shard_map/ppermute | solution.py:44
  125.6 13.9 %collective-permute-done.17 = bf16[512,512]{1,0:T(8,128)(2,1)S(1)} collective-permute-done((bf16[512,512]{1,0:T(8,128)(2,1)S(1)}, bf16[512,512]{1,0:T(8,128)(2,1)S(1)}, u32[]{:S(2)}, u32[]{:S(2)}) %collective-permute-start.17) | collective-permute-done | bytes 524320 | tf_op jit(solution)/shard_map/ppermute | solution.py:44
  139.5 1.7 %fusion.43 = bf16[512,512]{1,0:T(8,128)(2,1)S(1)} fusion(f32[512,512]{1,0:T(8,128)S(1)} %copy-done, bf16[512,512]{0,1:T(8,128)(2,1)S(1)} %bitcast.33, bf16[512,512]{1,0:T(8,128)(2,1)S(1)} %constant_dynamic-update-slice_fusion, bf16[512,512]{1,0:T(8,128)(2,1)} %collective-permute-done.18, bf16[512,512]{1,0:T(8,128)(2,1)S(1)} %collective-permute-done.17, ...), kind=kOutput, calls=%fused_computation.42 | convolution fusion | flops 270532608 | bytes 4194304 | tf_op jit(solution)/shard_map/dot_general | solution.py:103
  141.1 5.6 %collective-permute-done.11 = bf16[512,512]{1,0:T(8,128)(2,1)S(1)} collective-permute-done((bf16[512,512]{1,0:T(8,128)(2,1)S(1)}, bf16[512,512]{1,0:T(8,128)(2,1)S(1)}, u32[]{:S(2)}, u32[]{:S(2)}) %collective-permute-start.11) | collective-permute-done | bytes 524320 | tf_op jit(solution)/shard_map/ppermute | solution.py:44
  (79 shorter events, 18.0 us)
Async XLA Ops:
  0.0 45.4 %collective-permute-start = (bf16[2048,128]{1,0:T(8,128)(2,1)}, bf16[2048,128]{1,0:T(8,128)(2,1)}, u32[]{:S(2)}, u32[]{:S(2)}) collective-permute-start(bf16[2048,128]{1,0:T(8,128)(2,1)} %param.11), channel_id=1, source_target_pairs={{0,8},{4,12},{8,0},{12,4},{1,9},{5,13},{9,1},{13,5},{2,10},{6,14},... | collective-permute-start | bytes 1572872 | tf_op jit(solution)/shard_map/ppermute | solution.py:56
  2.9 41.7 %collective-permute-start.5 = (bf16[128,512]{1,0:T(8,128)(2,1)}, bf16[128,512]{1,0:T(8,128)(2,1)S(1)}, u32[]{:S(2)}, u32[]{:S(2)}) collective-permute-start(bf16[128,512]{1,0:T(8,128)(2,1)} %param.12), channel_id=1, source_target_pairs={{0,8},{4,12},{8,0},{12,4},{1,9},{5,13},{9,1},{13,5},{2,10},{6,14},... | collective-permute-start | bytes 393224 | tf_op jit(solution)/shard_map/ppermute | solution.py:56
  8.5 115.6 %collective-permute-start.18 = (bf16[512,512]{1,0:T(8,128)(2,1)S(1)}, bf16[512,512]{1,0:T(8,128)(2,1)}, u32[]{:S(2)}, u32[]{:S(2)}) collective-permute-start(bf16[512,512]{1,0:T(8,128)(2,1)S(1)} %fusion.89), channel_id=1, source_target_pairs={{0,1},{3,2},{4,5},{7,6},{8,9},{11,10},{12,13},{15,14},{16,17},{19,... | collective-permute-start | bytes 1572872 | tf_op jit(solution)/shard_map/ppermute | solution.py:44
  18.3 31.4 %collective-permute-start.15 = (bf16[512,512]{1,0:T(8,128)(2,1)}, bf16[512,512]{1,0:T(8,128)(2,1)}, u32[]{:S(2)}, u32[]{:S(2)}) collective-permute-start(bf16[512,512]{1,0:T(8,128)(2,1)} %fusion.79), channel_id=1, source_target_pairs={{0,1},{3,2},{4,5},{7,6},{8,9},{11,10},{12,13},{15,14},{16,17},{19,... | collective-permute-start | bytes 1572872 | tf_op jit(solution)/shard_map/ppermute | solution.py:44
  25.3 27.1 %collective-permute-start.13 = (bf16[512,512]{1,0:T(8,128)(2,1)}, bf16[512,512]{1,0:T(8,128)(2,1)}, u32[]{:S(2)}, u32[]{:S(2)}) collective-permute-start(bf16[512,512]{1,0:T(8,128)(2,1)} %fusion.99), channel_id=1, source_target_pairs={{0,1},{3,2},{4,5},{7,6},{8,9},{11,10},{12,13},{15,14},{16,17},{19,... | collective-permute-start | bytes 1572872 | tf_op jit(solution)/shard_map/ppermute | solution.py:44
  28.2 11.9 %slice-start = ((s8[8388608]{0:T(1024)(128)(4,1)}), s8[4194304]{0:T(1024)(128)(4,1)S(1)}, s32[]{:S(2)}) async-start(s8[8388608]{0:T(1024)(128)(4,1)} %bitcast.35), calls=%async_computation | async-start | bytes 8388608
  45.4 1.9 %collective-permute-start.6 = (bf16[256,512]{1,0:T(8,128)(2,1)}, bf16[256,512]{1,0:T(8,128)(2,1)}, u32[]{:S(2)}, u32[]{:S(2)}) collective-permute-start(bf16[256,512]{1,0:T(8,128)(2,1)} %pad_maximum_fusion.2), channel_id=1, source_target_pairs={{0,4},{4,0},{8,12},{12,8},{1,5},{5,1},{9,13},{13,9},{2,6},{6,2},{1... | collective-permute-start | bytes 786440 | tf_op jit(solution)/shard_map/ppermute | solution.py:56
  46.5 26.8 %collective-permute-start.1 = (bf16[2048,256]{1,0:T(8,128)(2,1)S(1)}, bf16[2048,256]{1,0:T(8,128)(2,1)}, u32[]{:S(2)}, u32[]{:S(2)}) collective-permute-start(bf16[2048,256]{1,0:T(8,128)(2,1)S(1)} %pad_maximum_fusion), channel_id=1, source_target_pairs={{0,4},{4,0},{8,12},{12,8},{1,5},{5,1},{9,13},{13,9},{2,6},{6,2},{1... | collective-permute-start | bytes 3145736 | tf_op jit(solution)/shard_map/ppermute | solution.py:56
  47.1 26.0 %copy-start.3 = (bf16[512,512]{1,0:T(8,128)(2,1)S(1)}, bf16[512,512]{1,0:T(8,128)(2,1)}, u32[]{:S(2)}) copy-start(bf16[512,512]{1,0:T(8,128)(2,1)} %fusion.74) | copy-start | bytes 1572868
  47.2 93.9 %collective-permute-start.12 = (bf16[512,512]{1,0:T(8,128)(2,1)}, bf16[512,512]{1,0:T(8,128)(2,1)S(1)}, u32[]{:S(2)}, u32[]{:S(2)}) collective-permute-start(bf16[512,512]{1,0:T(8,128)(2,1)} %fusion.84), channel_id=1, source_target_pairs={{0,1},{3,2},{4,5},{7,6},{8,9},{11,10},{12,13},{15,14},{16,17},{19,... | collective-permute-start | bytes 1572872 | tf_op jit(solution)/shard_map/ppermute | solution.py:44
  49.7 24.3 %copy-start.6 = (bf16[2048,128]{1,0:T(8,128)(2,1)S(1)}, bf16[2048,128]{1,0:T(8,128)(2,1)}, u32[]{:S(2)}) copy-start(bf16[2048,128]{1,0:T(8,128)(2,1)} %param.11) | copy-start | bytes 1572868
  49.7 22.8 %collective-permute-start.9 = (bf16[512,512]{1,0:T(8,128)(2,1)}, bf16[512,512]{1,0:T(8,128)(2,1)S(1)}, u32[]{:S(2)}, u32[]{:S(2)}) collective-permute-start(bf16[512,512]{1,0:T(8,128)(2,1)} %fusion.74), channel_id=1, source_target_pairs={{0,1},{3,2},{4,5},{7,6},{8,9},{11,10},{12,13},{15,14},{16,17},{19,... | collective-permute-start | bytes 1572872 | tf_op jit(solution)/shard_map/ppermute | solution.py:44
  52.5 30.6 %collective-permute-start.7 = (bf16[512,512]{1,0:T(8,128)(2,1)S(1)}, bf16[512,512]{1,0:T(8,128)(2,1)S(1)}, u32[]{:S(2)}, u32[]{:S(2)}) collective-permute-start(bf16[512,512]{1,0:T(8,128)(2,1)S(1)} %copy-done.2), channel_id=1, source_target_pairs={{0,1},{3,2},{4,5},{7,6},{8,9},{11,10},{12,13},{15,14},{16,17},{19,... | collective-permute-start | bytes 1572872 | tf_op jit(solution)/shard_map/ppermute | solution.py:44
  72.4 19.0 %collective-permute-start.16 = (bf16[512,512]{1,0:T(8,128)(2,1)S(1)}, bf16[512,512]{1,0:T(8,128)(2,1)S(1)}, u32[]{:S(2)}, u32[]{:S(2)}) collective-permute-start(bf16[512,512]{1,0:T(8,128)(2,1)S(1)} %add_convert_fusion.1), channel_id=1, source_target_pairs={{1,2},{2,1},{5,6},{6,5},{9,10},{10,9},{13,14},{14,13},{17,18},{18,... | collective-permute-start | bytes 1572872 | tf_op jit(solution)/shard_map/ppermute | solution.py:44
  73.3 52.3 %collective-permute-start.14 = (bf16[512,512]{1,0:T(8,128)(2,1)S(1)}, bf16[512,512]{1,0:T(8,128)(2,1)S(1)}, u32[]{:S(2)}, u32[]{:S(2)}) collective-permute-start(bf16[512,512]{1,0:T(8,128)(2,1)S(1)} %add_convert_fusion.2), channel_id=1, source_target_pairs={{1,2},{2,1},{5,6},{6,5},{9,10},{10,9},{13,14},{14,13},{17,18},{18,... | collective-permute-start | bytes 1572872 | tf_op jit(solution)/shard_map/ppermute | solution.py:44
  79.3 15.0 %copy-start.1 = (bf16[512,512]{1,0:T(8,128)(2,1)S(1)}, bf16[512,512]{1,0:T(8,128)(2,1)}, u32[]{:S(2)}) copy-start(bf16[512,512]{1,0:T(8,128)(2,1)} %fusion.84) | copy-start | bytes 1572868
  83.1 7.6 %collective-permute-start.2 = (bf16[1024,64]{0,1:T(8,128)(2,1)S(1)}, bf16[1024,64]{0,1:T(8,128)(2,1)S(1)}, u32[]{:S(2)}, u32[]{:S(2)}) collective-permute-start(bf16[1024,64]{0,1:T(8,128)(2,1)S(1)} %multiply_reduce_fusion), channel_id=1, source_target_pairs={{0,1},{3,2},{4,5},{7,6},{8,9},{11,10},{12,13},{15,14},{16,17},{19,... | collective-permute-start | bytes 393224 | tf_op jit(solution)/shard_map/ppermute | solution.py:44
  90.7 2.3 %collective-permute-start.10 = (bf16[512,512]{1,0:T(8,128)(2,1)S(1)}, bf16[512,512]{1,0:T(8,128)(2,1)S(1)}, u32[]{:S(2)}, u32[]{:S(2)}) collective-permute-start(bf16[512,512]{1,0:T(8,128)(2,1)S(1)} %add_convert_fusion.4), channel_id=1, source_target_pairs={{1,2},{2,1},{5,6},{6,5},{9,10},{10,9},{13,14},{14,13},{17,18},{18,... | collective-permute-start | bytes 1572872 | tf_op jit(solution)/shard_map/ppermute | solution.py:44
  91.5 0.8 collective-permute-start.3
  92.3 48.8 %collective-permute-start.8 = (bf16[512,512]{1,0:T(8,128)(2,1)S(1)}, bf16[512,512]{1,0:T(8,128)(2,1)S(1)}, u32[]{:S(2)}, u32[]{:S(2)}) collective-permute-start(bf16[512,512]{1,0:T(8,128)(2,1)S(1)} %add_convert_fusion.5), channel_id=1, source_target_pairs={{1,2},{2,1},{5,6},{6,5},{9,10},{10,9},{13,14},{14,13},{17,18},{18,... | collective-permute-start | bytes 1572872 | tf_op jit(solution)/shard_map/ppermute | solution.py:44
  93.1 29.7 %collective-permute-start.4 = (bf16[1024,64]{0,1:T(8,128)(2,1)S(1)}, bf16[1024,64]{0,1:T(8,128)(2,1)S(1)}, u32[]{:S(2)}, u32[]{:S(2)}) collective-permute-start(bf16[1024,64]{0,1:T(8,128)(2,1)S(1)} %add_convert_fusion.6), channel_id=1, source_target_pairs={{2,3},{1,0},{6,7},{5,4},{10,11},{9,8},{14,15},{13,12},{18,19},{17,... | collective-permute-start | bytes 393224 | tf_op jit(solution)/shard_map/ppermute | solution.py:44
  94.5 45.0 %copy-start = (f32[512,512]{1,0:T(8,128)S(1)}, f32[512,512]{1,0:T(8,128)}, u32[]{:S(2)}) copy-start(f32[512,512]{1,0:T(8,128)} %fusion.22) | copy-start | bytes 3145732
  122.7 16.7 %collective-permute-start.17 = (bf16[512,512]{1,0:T(8,128)(2,1)S(1)}, bf16[512,512]{1,0:T(8,128)(2,1)S(1)}, u32[]{:S(2)}, u32[]{:S(2)}) collective-permute-start(bf16[512,512]{1,0:T(8,128)(2,1)S(1)} %add_convert_fusion), channel_id=1, source_target_pairs={{2,3},{1,0},{6,7},{5,4},{10,11},{9,8},{14,15},{13,12},{18,19},{17,... | collective-permute-start | bytes 1572872 | tf_op jit(solution)/shard_map/ppermute | solution.py:44
  124.2 22.6 %collective-permute-start.11 = (bf16[512,512]{1,0:T(8,128)(2,1)S(1)}, bf16[512,512]{1,0:T(8,128)(2,1)S(1)}, u32[]{:S(2)}, u32[]{:S(2)}) collective-permute-start(bf16[512,512]{1,0:T(8,128)(2,1)S(1)} %add_convert_fusion.3), channel_id=1, source_target_pairs={{2,3},{1,0},{6,7},{5,4},{10,11},{9,8},{14,15},{13,12},{18,19},{17,... | collective-permute-start | bytes 1572872 | tf_op jit(solution)/shard_map/ppermute | solution.py:44
  (9 other events, 35.4 us)

commit v2 on v0

v2 whole, which is shorter than its diff:
```python
import functools

import jax
import jax.numpy as jnp
from jax import lax
from jax.experimental import pallas as pl
from jax.experimental.pallas import tpu as pltpu
from jax.sharding import PartitionSpec as P

F32 = jnp.float32
BF16 = jnp.bfloat16
LANES = 128
PIECES = 4
ANY = pl.BlockSpec(memory_space=pl.ANY)
VMEM = pl.BlockSpec(memory_space=pltpu.VMEM)
PARAMS = pltpu.CompilerParams(vmem_limit_bytes=64 * 1024 * 1024 - 128 * 1024)
COST = pl.CostEstimate(flops=1, bytes_accessed=1, transcendentals=0)


def call(kernel, outs, in_specs, scratch, token, *args, out_specs, aliases=None):
    n_in, n_out = len(args), len(outs)
    aliases = dict(aliases or {})
    if token is not None:
        args += (token,)
        in_specs = [*in_specs, ANY]
        aliases[n_in] = n_out

    def body(*refs):
        given = refs[:n_in]
        rest = refs[len(args) :]
        kernel(*given, *rest[:n_out], *rest[n_out + 1 :])

    return pl.pallas_call(
        body,
        out_shape=(*outs, jax.ShapeDtypeStruct((8, LANES), F32)),
        in_specs=in_specs,
        out_specs=(*out_specs, ANY),
        scratch_shapes=scratch,
        input_output_aliases=aliases,
        compiler_params=PARAMS,
        cost_estimate=COST,
    )(*args)


def relay(token, *arrays):
    return call(
        lambda *refs: None,
        [jax.ShapeDtypeStruct(a.shape, a.dtype) for a in arrays],
        [ANY] * len(arrays),
        [],
        token,
        *arrays,
        out_specs=[ANY] * len(arrays),
        aliases={i: i for i in range(len(arrays))},
    )


def in_middle():
    me = lax.axis_index("tensor")
    return jnp.logical_and(me > 0, me < 3)


def block_of(phase):
    me = lax.axis_index("tensor")
    if phase == 0:
        return jnp.where(me < 2, 3, 0)
    if phase == 1:
        return jnp.where(me < 2, 2, 1)
    if phase == 2:
        return me + 1 - 2 * lax.rem(me, 2)
    return me


def copy_in(pairs, sems):
    copies = [pltpu.make_async_copy(a, b, sems.at[i]) for i, (a, b) in enumerate(pairs)]
    for c in copies:
        c.start()
    return copies


def fetch(hidden, weight, lo, rows, phase, h_buf, w_buf, h_sem, w_sem):
    depth, cols = w_buf.shape
    step = depth // PIECES
    first = pl.multiple_of(block_of(phase) * cols, cols)
    h_copies, w_copies = [], []
    for k in range(PIECES):
        span = pl.ds(k * step, step)
        if h_sem is not None:
            pair = (hidden.at[pl.ds(lo, rows), span], h_buf.at[pl.ds(lo, rows), span])
            h_copies += copy_in([pair], h_sem.at[pl.ds(k, 1)])
        pair = (weight.at[span, pl.ds(first, cols)], w_buf.at[span])
        w_copies += copy_in([pair], w_sem.at[pl.ds(k, 1)])
    return h_copies, w_copies


def product(h_buf, w_buf, lo, rows, copies):
    h_copies, w_copies = copies
    step = w_buf.shape[0] // PIECES
    total = None
    for k in range(PIECES):
        if h_copies:
            h_copies[k].wait()
        if w_copies:
            w_copies[k].wait()
        span = pl.ds(k * step, step)
        term = jnp.dot(h_buf[pl.ds(lo, rows), span], w_buf[span], preferred_element_type=F32)
        total = term if total is None else total + term
    return total


def first_kernel(rows, hidden, weight, out, h_buf, w_buf, h_sem, w_sem):
    copies = fetch(hidden, weight, 0, rows, 0, h_buf, w_buf, h_sem, w_sem)
    out[...] = product(h_buf, w_buf, 0, rows, copies).astype(BF16)


def first_product(hidden, weight, rows):
    depth, cols = hidden.shape[1], weight.shape[1] // 4
    return call(
        functools.partial(first_kernel, rows),
        [jax.ShapeDtypeStruct((rows, cols), BF16)],
        [ANY] * 2,
        [
            pltpu.VMEM((rows, depth), BF16),
            pltpu.VMEM((depth, cols), BF16),
            pltpu.SemaphoreType.DMA((PIECES,)),
            pltpu.SemaphoreType.DMA((PIECES,)),
        ],
        None,
        hidden,
        weight,
        out_specs=[VMEM],
    )


def next_kernel(start, hidden, weight, p0, p1a, p1b, p2, h_buf, w0, w1, w2, buf, h_sem, w_sem, o_sem):
    rows = hidden.shape[0]
    half = rows // 2
    copies0 = fetch(hidden, weight, start, rows - start, 0, h_buf, w0, h_sem.at[0], w_sem.at[0])
    if start:
        early = copy_in([(hidden.at[pl.ds(0, start)], h_buf.at[pl.ds(0, start)])], h_sem.at[1])
    copies1 = fetch(hidden, weight, 0, rows, 1, h_buf, w1, None, w_sem.at[1])
    copies2 = fetch(hidden, weight, 0, rows, 2, h_buf, w2, None, w_sem.at[2])
    buf[0, pl.ds(start, rows - start)] = product(h_buf, w0, start, rows - start, copies0).astype(BF16)
    outs = copy_in([(buf.at[0, pl.ds(start, rows - start)], p0)], o_sem.at[pl.ds(0, 1)])
    for c in early:
        c.wait()
    buf[1] = product(h_buf, w1, 0, rows, copies1).astype(BF16)
    outs += copy_in(
        [(buf.at[1, pl.ds(0, half)], p1a), (buf.at[1, pl.ds(half, half)], p1b)],
        o_sem.at[pl.ds(1, 2)],
    )
    buf[2] = product(h_buf, w2, 0, rows, copies2).astype(BF16)
    outs += copy_in([(buf.at[2], p2)], o_sem.at[pl.ds(3, 1)])
    for c in outs:
        c.wait()


def next_products(token, hidden, weight, start):
    rows, depth = hidden.shape
    cols = weight.shape[1] // 4
    shapes = [(rows - start, cols), (rows // 2, cols), (rows // 2, cols), (rows, cols)]
    return call(
        functools.partial(next_kernel, start),
        [jax.ShapeDtypeStruct(shape, BF16) for shape in shapes],
        [ANY] * 2,
        [
            pltpu.VMEM((rows, depth), BF16),
            pltpu.VMEM((depth, cols), BF16),
            pltpu.VMEM((depth, cols), BF16),
            pltpu.VMEM((depth, cols), BF16),
            pltpu.VMEM((3, rows, cols), BF16),
            pltpu.SemaphoreType.DMA((2, PIECES)),
            pltpu.SemaphoreType.DMA((3, PIECES)),
            pltpu.SemaphoreType.DMA((4,)),
        ],
        token,
        hidden,
        weight,
        out_specs=[ANY] * 4,
    )


def add_kernel(a, b, out):
    out[...] = (a[...].astype(F32) + b[...].astype(F32)).astype(BF16)


def add(token, a, b):
    out = jax.ShapeDtypeStruct(a.shape, BF16)
    return call(add_kernel, [out], [VMEM, VMEM], [], token, a, b, out_specs=[VMEM])


def add_middle_kernel(p, lo, hi, out):
    cut = lo.shape[0]
    middle = in_middle()
    for rows, b in ((pl.ds(0, cut), lo), (pl.ds(cut, hi.shape[0]), hi)):
        out[rows] = (p[rows].astype(F32) + jnp.where(middle, b[...].astype(F32), 0.0)).astype(BF16)


def add_middle(token, p, lo, hi):
    out = jax.ShapeDtypeStruct(p.shape, p.dtype)
    return call(add_middle_kernel, [out], [VMEM] * 3, [], token, p, lo, hi, out_specs=[VMEM])


def low_kernel(hidden, y0, y1, y2, y3, code, out, h_buf, w_buf, acc, h_sem, w_sem):
    rows, depth = hidden.shape
    step = depth // PIECES
    h_copies, w_copies = [], []
    for k in range(PIECES):
        span = pl.ds(k * step, step)
        h_copies += copy_in([(hidden.at[:, span], h_buf.at[:, span])], h_sem.at[pl.ds(k, 1)])
        for p, y in enumerate((y0, y1, y2, y3)):
            pair = (y.at[span], w_buf.at[span, pl.ds(p * LANES, LANES)])
            w_copies += copy_in([pair], w_sem.at[pl.ds(4 * k + p, 1)])
    for k in range(PIECES):
        h_copies[k].wait()
        for p in range(4):
            w_copies[4 * k + p].wait()
        span = pl.ds(k * step, step)
        product = jnp.dot(h_buf[:, span], w_buf[span], preferred_element_type=F32)
        if k == 0:
            acc[...] = product
        else:
            acc[...] += product
    half = rows // 2
    width = LANES // 2
    tile = min(256, half)
    owner = lax.broadcasted_iota(jnp.int32, (tile, 4 * LANES), 1) // width
    lane = lax.broadcasted_iota(jnp.int32, (tile, LANES), 1)

    def own_columns(at):
        mine = jnp.where(owner == code[at] // LANES, acc[at], 0.0)
        both = mine[:, :LANES]
        for p in range(1, 4):
            both = both + mine[:, p * LANES : (p + 1) * LANES]
        return both + pltpu.roll(both, width, 1)

    for t in range(half // tile):
        upper, lower = own_columns(pl.ds(t * tile, tile)), own_columns(pl.ds(half + t * tile, tile))
        out[pl.ds(t * tile, tile)] = jnp.where(lane < width, upper, lower).astype(BF16)


def low_product(token, hidden, ys, code):
    rows, depth = hidden.shape
    return call(
        low_kernel,
        [jax.ShapeDtypeStruct((rows // 2, LANES), BF16)],
        [ANY] * 5 + [VMEM],
        [
            pltpu.VMEM((rows, depth), BF16),
            pltpu.VMEM((depth, 4 * LANES), BF16),
            pltpu.VMEM((rows, 4 * LANES), F32),
            pltpu.SemaphoreType.DMA((PIECES,)),
            pltpu.SemaphoreType.DMA((4 * PIECES,)),
        ],
        token,
        hidden,
        *ys,
        code,
        out_specs=[VMEM],
    )


def up_kernel(hidden, weight, low, outer, y0, y1, y2, y3, code, out, h_buf, w_buf, u_buf, h_sem, w_sem, sem):
    rows, cols = out.shape
    copies = fetch(hidden, weight, 0, rows, 3, h_buf, w_buf, h_sem, w_sem)
    ups = copy_in([(y, u_buf.at[pl.ds(p * LANES, LANES)]) for p, y in enumerate((y0, y1, y2, y3))], sem)
    out[...] = product(h_buf, w_buf, 0, rows, copies)
    for c in ups:
        c.wait()
    middle = in_middle()
    width = LANES // 2
    half = rows // 2
    tile = min(256, half)
    column = lax.broadcasted_iota(jnp.int32, (tile, 4 * LANES), 1) // width
    lane = lax.broadcasted_iota(jnp.int32, (tile, LANES), 1)
    for t in range(rows // tile):
        at = pl.ds(t * tile, tile)
        hi = t * tile >= half
        packed = pl.ds(t * tile - (half if hi else 0), tile)
        mine = jnp.where(middle, low[packed].astype(F32), outer[packed].astype(F32))
        turned = pltpu.roll(mine, width, 1)
        mine = jnp.where(lane < width, turned, mine) if hi else jnp.where(lane < width, mine, turned)
        live = lax.rem(code[at], LANES)
        mine = mine * (width / (2.0 * live.astype(F32)))
        mine = jnp.where(lax.rem(lane, width) < live, mine, 0.0)
        spread = jnp.concatenate([mine] * 4, axis=1)
        spread = jnp.where(column == code[at] // LANES, spread, 0.0).astype(BF16)
        out[at] += jnp.dot(spread, u_buf[...], preferred_element_type=F32)


def own_and_up(token, hidden, weight, low, outer, ys, code):
    rows, depth = hidden.shape
    cols = weight.shape[1] // 4
    return call(
        up_kernel,
        [jax.ShapeDtypeStruct((rows, cols), F32)],
        [ANY] * 2 + [VMEM] * 2 + [ANY] * 4 + [VMEM],
        [
            pltpu.VMEM((rows, depth), BF16),
            pltpu.VMEM((depth, cols), BF16),
            pltpu.VMEM((4 * LANES, cols), BF16),
            pltpu.SemaphoreType.DMA((PIECES,)),
            pltpu.SemaphoreType.DMA((PIECES,)),
            pltpu.SemaphoreType.DMA((4,)),
        ],
        token,
        hidden,
        weight,
        low,
        outer,
        *ys,
        code,
        out_specs=[VMEM],
    )


def inner_kernel(total, lo, hi, out):
    cut = lo.shape[0]
    middle = in_middle()
    for rows, b in ((pl.ds(0, cut), lo), (pl.ds(cut, hi.shape[0]), hi)):
        out[rows] = total[rows] + jnp.where(middle, b[...].astype(F32), 0.0)


def inner_sum(token, total, lo, hi):
    out = jax.ShapeDtypeStruct(total.shape, F32)
    return call(inner_kernel, [out], [VMEM] * 3, [], token, total, lo, hi, out_specs=[VMEM])


def last_kernel(total, m, out):
    out[...] = (total[...] + m[...].astype(F32)).astype(BF16)


def last_sum(token, total, m):
    out = jax.ShapeDtypeStruct(total.shape, BF16)
    return call(last_kernel, [out], [VMEM] * 2, [], token, total, m, out_specs=[VMEM])[0]


def by_adapter(row_adapter, values):
    every = jnp.arange(values.shape[0], dtype=jnp.int32)
    return jnp.sum(jnp.where(row_adapter == every[None, :], values[None, :], 0), axis=1, keepdims=True)


def line_of_four(hidden, weight, down, up, row_adapter, rank_of_adapter, adapter_storage_slot):
    rows = hidden.shape[0]
    start = rows // 2
    at = lax.axis_index("dp")
    per_index = adapter_storage_slot.shape[0] // 4

    def cross(v):
        return lax.ppermute(v, "tensor", [(0, 1), (1, 0), (2, 3), (3, 2)])

    def inner(v):
        return lax.ppermute(v, "tensor", [(1, 2), (2, 1)])

    def swap(v, bit):
        return lax.ppermute(v, "dp", [(i, i ^ bit) for i in range(4)])

    places = ((adapter_storage_slot // per_index) ^ at) * per_index + adapter_storage_slot % per_index
    code = by_adapter(row_adapter, places * LANES + rank_of_adapter)

    down2, down1 = swap(down, 2), swap(down, 1)
    up2, up1 = swap(up, 2), swap(up, 1)

    p0a, t = first_product(hidden, weight, start)
    a1a = cross(p0a)
    p0b, p1a, p1b, p2, t = next_products(t, hidden, weight, start)
    a1b = cross(p0b)
    a2a = cross(p1a)
    v, t = add(t, p0a, a1a)
    b1a = inner(v)
    down2, up2, t = relay(t, down2, up2)
    downs = (down, down1, down2, swap(down2, 1))
    ups = (up, up1, up2, swap(up2, 1))
    low, t = low_product(t, hidden, downs, code)
    e1 = cross(low)
    p1b, t = relay(t, p1b)
    a2b = cross(p1b)
    v, t = add(t, p0b, a1b)
    b1b = inner(v)
    low, t = add(t, low, e1)
    e2 = inner(low)
    v, t = add(t, p1a, a2a)
    b2a = inner(v)
    v, t = add_middle(t, p2, b1a, b1b)
    m3 = cross(v)
    low, t = add(t, low, e2)
    e3 = cross(low)
    v, t = add(t, p1b, a2b)
    b2b = inner(v)
    total, t = own_and_up(t, hidden, weight, low, e3, ups, code)
    total, t = inner_sum(t, total, b2a, b2b)
    return last_sum(t, total, m3)


def any_line(hidden, weight, down, up, row_adapter, rank_of_adapter, adapter_storage_slot):
    rows = hidden.shape[0]
    adapters = rank_of_adapter.shape[0]
    width = down.shape[1] * lax.axis_size("dp") // adapters
    slot = by_adapter(row_adapter, adapter_storage_slot)
    rank = by_adapter(row_adapter, rank_of_adapter)
    chosen = slot == jnp.arange(adapters, dtype=jnp.int32)[None, :]
    partial = jnp.dot(hidden, weight, preferred_element_type=F32).astype(BF16)
    base = lax.psum_scatter(partial, "tensor", scatter_dimension=1, tiled=True).astype(F32)
    downs = lax.all_gather(down, "dp", axis=1, tiled=True)
    product = jnp.dot(hidden, downs, preferred_element_type=F32)
    low = jnp.einsum("rac,ra->rc", product.reshape(rows, adapters, width), chosen.astype(F32))
    low = lax.psum(low.astype(BF16), "tensor").astype(F32)
    live = jnp.arange(width, dtype=jnp.int32)[None, :] < rank
    scaling = width / (2.0 * rank.astype(F32))
    low_rank = jnp.where(live, low * scaling, F32(0.0)).astype(BF16)
    spread = jnp.where(chosen[:, :, None], low_rank[:, None, :], jnp.zeros((), BF16)).reshape(rows, -1)
    ups = lax.all_gather(up, "dp", axis=0, tiled=True)
    return (base + jnp.dot(spread, ups, preferred_element_type=F32)).astype(BF16)


def on_device(hidden, weight, down, up, *rest):
    fits = (
        lax.axis_size("tensor") == 4
        and lax.axis_size("dp") == 4
        and down.shape[1] == LANES
        and up.shape[0] == LANES
        and rest[1].shape[0] == 8
        and hidden.shape[0] % 512 == 0
        and hidden.shape[1] % (PIECES * LANES) == 0
        and up.shape[1] == 4 * LANES
    )
    return (line_of_four if fits else any_line)(hidden, weight, down, up, *rest)


def solution(mesh):
    return jax.shard_map(
        on_device,
        mesh=mesh,
        in_specs=(
            P(("groups", "dp"), "tensor"),
            P("tensor", None),
            P("tensor", "dp"),
            P("dp", "tensor"),
            P(("groups", "dp"), None),
            P(),
            P(),
        ),
        out_specs=P(("groups", "dp"), "tensor"),
        check_vma=False,
    )
```

time: 164 us -> 103 us (0.63)
  waiting for transfers between devices: 118 us -> 23.8 us
  Pallas kernels: 0 us -> 49.4 us
  starting transfers between devices: 0.08 us -> 28.5 us
  matrix products: 22 us -> 0 us
  between operations: 13.1 us -> 0.11 us
  blocking collectives: 7.19 us -> 0 us
  other arithmetic: 2.72 us -> 0.1 us
    reduce_scatter x1 -> x0, waiting for transfers between devices: 77.8 us -> none  [on_device(): lax.psum_scatter(partial_sum.astype(jnp.bfloat16), 'tensor', scatter_dime...]
    pallas_call x0 -> x15, Pallas kernels: none -> 49.4 us  [call(): pl.pallas_call(body, out_shape=(*outs, jax.ShapeDtypeStruct((8, LANES), F...]
    ppermute x0 -> x18, starting transfers between devices: none -> 28.5 us  [the longest x7 18.8 us: cross(): return lax.ppermute(v, 'tensor', [(0, 1), (1, 0), (2, 3), (3, 2)])]
    all_gather x1 -> x0, waiting for transfers between devices: 26.4 us -> none  [on_device(): lax.all_gather(adapter_down_factors, 'dp', axis=1, tiled=True)]
    ppermute x0 -> x18, waiting for transfers between devices: none -> 23.8 us  [the longest x7 20.6 us: cross(): return lax.ppermute(v, 'tensor', [(0, 1), (1, 0), (2, 3), (3, 2)])]
    dot_general x3 -> x0, matrix products: 22 us -> none  [the longest x1 13.8 us: on_device(): jnp.dot(hidden, key_value_weight, preferred_element_type=jnp.float32)]
    psum x1 -> x0, waiting for transfers between devices: 12.6 us -> none  [on_device(): lax.psum(low_part.astype(jnp.bfloat16), 'tensor').astype(jnp.float32)]
    all_gather x1 -> x0, blocking collectives: 7.19 us -> none  [on_device(): lax.all_gather(adapter_up_factors, 'dp', axis=0, tiled=True)]
  transfers between devices with their start and end apart: 3 -> 18, of which waited for: 3 -> 5; matrix products, arithmetic and copies ran while one was open for 10% -> 1% of each run, Pallas kernels for 0% -> 41%
where the time goes in v2:
time: 103 us
  Pallas kernels  49.4 us (48%)
  starting transfers between devices  28.5 us (28%)
  waiting for transfers between devices  23.8 us (23%)
  local copies, waits for them, and re-layouts  1.05 us (1%)
    pallas_call x15, Pallas kernels, call(): pl.pallas_call(body, out_shape=(*outs, jax.ShapeDtypeStruct((8, LANES), F...  49.4 us
    ppermute x7, waiting for transfers between devices, cross(): return lax.ppermute(v, 'tensor', [(0, 1), (1, 0), (2, 3), (3, 2)])  20.6 us
    ppermute x7, starting transfers between devices, cross(): return lax.ppermute(v, 'tensor', [(0, 1), (1, 0), (2, 3), (3, 2)])  18.8 us
    ppermute x5, starting transfers between devices, inner(): return lax.ppermute(v, 'tensor', [(1, 2), (2, 1)])  7.12 us
    ppermute x6, waiting for transfers between devices, swap(): return lax.ppermute(v, 'dp', [(i, i ^ bit) for i in range(4)])  3.18 us
    ppermute x6, starting transfers between devices, swap(): return lax.ppermute(v, 'dp', [(i, i ^ bit) for i in range(4)])  2.54 us
  transfers between devices with their start and end apart: 18, of which 5 were waited for; matrix products, arithmetic and copies ran while one was open for 1% of the time, Pallas kernels for 41%

profile of v2, /device:TPU:0, one launch (start us, length us, event | category | flops | bytes accessed | tf_op | source)
XLA Modules:
  0.0 102.9 jit_solution(15553988726034923026)
XLA Ops:
  0.0 3.9 %shard_map.73 = (bf16[512,512]{1,0:T(8,128)(2,1)}, f32[8,128]{1,0:T(8,128)}) custom-call(bf16[1024,2048]{1,0:T(8,128)(2,1)} %refs_0_.7, bf16[2048,2048]{1,0:T(8,128)(2,1)} %refs_1_.7), custom_call_target="tpu_custom_call" | custom-call | flops 1 | bytes 1 | tf_op jit(solution)/shard_map/pallas_call | solution.py:33
  3.9 3.1 %collective-permute-start.3 = (bf16[512,512]{1,0:T(8,128)(2,1)}, bf16[512,512]{1,0:T(8,128)(2,1)}, u32[]{:S(2)}, u32[]{:S(2)}) collective-permute-start(bf16[512,512]{1,0:T(8,128)(2,1)} %get-tuple-element.38.refs_0_), channel_id=1, source_target_pairs={{0,1},{1,0},{2,3},{3,2},{4,5},{5,4},{6,7},{7,6},{8,9},{9,8},{10,11... | collective-permute-start | bytes 1572872 | tf_op jit(solution)/shard_map/ppermute | solution.py:350
  7.0 1.5 %collective-permute-start.1 = (bf16[2048,128]{1,0:T(8,128)(2,1)}, bf16[2048,128]{1,0:T(8,128)(2,1)}, u32[]{:S(2)}, u32[]{:S(2)}) collective-permute-start(bf16[2048,128]{1,0:T(8,128)(2,1)} %refs_1_.6), channel_id=1, source_target_pairs={{0,8},{4,12},{8,0},{12,4},{1,9},{5,13},{9,1},{13,5},{2,10},{6,14},... | collective-permute-start | bytes 1572872 | tf_op jit(solution)/shard_map/ppermute | solution.py:356
  9.1 10.3 %shard_map.74 = (bf16[512,512]{1,0:T(8,128)(2,1)}, bf16[512,512]{1,0:T(8,128)(2,1)}, bf16[512,512]{1,0:T(8,128)(2,1)}, bf16[1024,512]{1,0:T(8,128)(2,1)}, f32[8,128]{1,0:T(8,128)}) custom-call(bf16[1024,2048]{1,0:T(8,128)(2,1)} %refs_0_.7, bf16[2048,2048]{1,0:T(8,128)(2,1)} %refs_1_.7, ...), custom_call_target="tpu_custom_call", output_to_operand_aliasing={{4}: (2, {})} | custom-call | flops 1 | bytes 1 | tf_op jit(solution)/shard_map/pallas_call | solution.py:33
  19.4 2.1 %shard_map.75 = (bf16[512,512]{1,0:T(8,128)(2,1)}, f32[8,128]{1,0:T(8,128)}) custom-call(bf16[512,512]{1,0:T(8,128)(2,1)} %get-tuple-element.38.refs_0_, bf16[512,512]{1,0:T(8,128)(2,1)} %collective-permute-done.3.refs_1_, f32[8,128]{1,0:T(8,128)} %get-tuple-element.40.refs_2_), custom_call_target="tpu_custom_call", output_to_operand_aliasing={{1}: (2, {})} | custom-call | flops 1 | bytes 1 | tf_op jit(solution)/shard_map/pallas_call | solution.py:33
  21.5 2.0 %collective-permute-done.2.refs_1_ = bf16[128,512]{1,0:T(8,128)(2,1)} collective-permute-done((bf16[128,512]{1,0:T(8,128)(2,1)}, bf16[128,512]{1,0:T(8,128)(2,1)}, u32[]{:S(2)}, u32[]{:S(2)}) %collective-permute-start.2) | collective-permute-done | bytes 131104 | tf_op jit(solution)/shard_map/ppermute | solution.py:356
  23.9 1.7 %collective-permute-start.10 = (bf16[512,512]{1,0:T(8,128)(2,1)}, bf16[512,512]{1,0:T(8,128)(2,1)}, u32[]{:S(2)}, u32[]{:S(2)}) collective-permute-start(bf16[512,512]{1,0:T(8,128)(2,1)} %get-tuple-element.54.refs_0_), channel_id=1, source_target_pairs={{0,1},{1,0},{2,3},{3,2},{4,5},{5,4},{6,7},{7,6},{8,9},{9,8},{10,11... | collective-permute-start | bytes 1572872 | tf_op jit(solution)/shard_map/ppermute | solution.py:350
  26.8 1.5 %collective-permute-start.8 = (bf16[512,512]{1,0:T(8,128)(2,1)}, bf16[512,512]{1,0:T(8,128)(2,1)}, u32[]{:S(2)}, u32[]{:S(2)}) collective-permute-start(bf16[512,512]{1,0:T(8,128)(2,1)} %get-tuple-element.52), channel_id=1, source_target_pairs={{1,2},{2,1},{5,6},{6,5},{9,10},{10,9},{13,14},{14,13},{17,18},{18,... | collective-permute-start | bytes 1572872 | tf_op jit(solution)/shard_map/ppermute | solution.py:353
  28.2 6.4 %shard_map.77 = (bf16[512,128]{1,0:T(8,128)(2,1)}, f32[8,128]{1,0:T(8,128)}) custom-call(bf16[1024,2048]{1,0:T(8,128)(2,1)} %refs_0_.7, bf16[2048,128]{1,0:T(8,128)(2,1)} %refs_1_.6, bf16[2048,128]{1,0:T(8,128)(2,1)} %collective-permute-done.refs_2_, bf16[2048,128]{1,0:T(8,128)(2,1)} %get-tuple-element.42.refs_3_, ...), custom_call_target="tpu_custom_call", output_to_operand_aliasing={{1}: (6, {})} | custom-call | flops 1 | bytes 1 | tf_op jit(solution)/shard_map/pallas_call | solution.py:33
  34.6 4.0 %collective-permute-done.6.refs_1_ = bf16[512,512]{1,0:T(8,128)(2,1)} collective-permute-done((bf16[512,512]{1,0:T(8,128)(2,1)}, bf16[512,512]{1,0:T(8,128)(2,1)}, u32[]{:S(2)}, u32[]{:S(2)}) %collective-permute-start.6) | collective-permute-done | bytes 524320 | tf_op jit(solution)/shard_map/ppermute | solution.py:350
  38.6 2.1 %shard_map.79 = (bf16[512,512]{1,0:T(8,128)(2,1)}, f32[8,128]{1,0:T(8,128)}) custom-call(bf16[512,512]{1,0:T(8,128)(2,1)} %get-tuple-element.45.refs_0_, bf16[512,512]{1,0:T(8,128)(2,1)} %collective-permute-done.6.refs_1_, f32[8,128]{1,0:T(8,128)} %get-tuple-element.48.refs_2_), custom_call_target="tpu_custom_call", output_to_operand_aliasing={{1}: (2, {})} | custom-call | flops 1 | bytes 1 | tf_op jit(solution)/shard_map/pallas_call | solution.py:33
  42.2 3.7 %collective-permute-start.5 = (bf16[512,128]{1,0:T(8,128)(2,1)}, bf16[512,128]{1,0:T(8,128)(2,1)}, u32[]{:S(2)}, u32[]{:S(2)}) collective-permute-start(bf16[512,128]{1,0:T(8,128)(2,1)} %get-tuple-element.44.refs_0_), channel_id=1, source_target_pairs={{0,1},{1,0},{2,3},{3,2},{4,5},{5,4},{6,7},{7,6},{8,9},{9,8},{10,11... | collective-permute-start | bytes 393224 | tf_op jit(solution)/shard_map/ppermute | solution.py:350
  46.0 6.7 %collective-permute-done.5.refs_1_ = bf16[512,128]{1,0:T(8,128)(2,1)} collective-permute-done((bf16[512,128]{1,0:T(8,128)(2,1)}, bf16[512,128]{1,0:T(8,128)(2,1)}, u32[]{:S(2)}, u32[]{:S(2)}) %collective-permute-start.5) | collective-permute-done | bytes 131104 | tf_op jit(solution)/shard_map/ppermute | solution.py:350
  52.7 1.7 %shard_map.80 = (bf16[512,128]{1,0:T(8,128)(2,1)}, f32[8,128]{1,0:T(8,128)}) custom-call(bf16[512,128]{1,0:T(8,128)(2,1)} %get-tuple-element.44.refs_0_, bf16[512,128]{1,0:T(8,128)(2,1)} %collective-permute-done.5.refs_1_, f32[8,128]{1,0:T(8,128)} %get-tuple-element.49.refs_2_), custom_call_target="tpu_custom_call", output_to_operand_aliasing={{1}: (2, {})} | custom-call | flops 1 | bytes 1 | tf_op jit(solution)/shard_map/pallas_call | solution.py:33
  54.3 2.1 %shard_map.81 = (bf16[512,512]{1,0:T(8,128)(2,1)}, f32[8,128]{1,0:T(8,128)}) custom-call(bf16[512,512]{1,0:T(8,128)(2,1)} %get-tuple-element.54.refs_0_, bf16[512,512]{1,0:T(8,128)(2,1)} %collective-permute-done.10.refs_1_, f32[8,128]{1,0:T(8,128)} %get-tuple-element.55.refs_2_), custom_call_target="tpu_custom_call", output_to_operand_aliasing={{1}: (2, {})} | custom-call | flops 1 | bytes 1 | tf_op jit(solution)/shard_map/pallas_call | solution.py:33
  56.5 2.9 %shard_map.82 = (bf16[1024,512]{1,0:T(8,128)(2,1)}, f32[8,128]{1,0:T(8,128)}) custom-call(bf16[1024,512]{1,0:T(8,128)(2,1)} %get-tuple-element.51.refs_0_, bf16[512,512]{1,0:T(8,128)(2,1)} %collective-permute-done.8.refs_1_, bf16[512,512]{1,0:T(8,128)(2,1)} %collective-permute-done.9.refs_2_, ...), custom_call_target="tpu_custom_call", output_to_operand_aliasing={{1}: (3, {})} | custom-call | flops 1 | bytes 1 | tf_op jit(solution)/shard_map/pallas_call | solution.py:33
  61.6 1.5 %collective-permute-start.15 = (bf16[512,512]{1,0:T(8,128)(2,1)}, bf16[512,512]{1,0:T(8,128)(2,1)}, u32[]{:S(2)}, u32[]{:S(2)}) collective-permute-start(bf16[512,512]{1,0:T(8,128)(2,1)} %get-tuple-element.64), channel_id=1, source_target_pairs={{1,2},{2,1},{5,6},{6,5},{9,10},{10,9},{13,14},{14,13},{17,18},{18,... | collective-permute-start | bytes 1572872 | tf_op jit(solution)/shard_map/ppermute | solution.py:353
  63.0 1.6 %shard_map.83 = (bf16[512,128]{1,0:T(8,128)(2,1)}, f32[8,128]{1,0:T(8,128)}) custom-call(bf16[512,128]{1,0:T(8,128)(2,1)} %get-tuple-element.50.refs_0_, bf16[512,128]{1,0:T(8,128)(2,1)} %collective-permute-done.7.refs_1_, f32[8,128]{1,0:T(8,128)} %get-tuple-element.57.refs_2_), custom_call_target="tpu_custom_call", output_to_operand_aliasing={{1}: (2, {})} | custom-call | flops 1 | bytes 1 | tf_op jit(solution)/shard_map/pallas_call | solution.py:33
  64.7 2.1 %shard_map.84 = (bf16[512,512]{1,0:T(8,128)(2,1)}, f32[8,128]{1,0:T(8,128)}) custom-call(bf16[512,512]{1,0:T(8,128)(2,1)} %get-tuple-element.60.refs_0_, bf16[512,512]{1,0:T(8,128)(2,1)} %collective-permute-done.14.refs_1_, f32[8,128]{1,0:T(8,128)} %get-tuple-element.61.refs_2_), custom_call_target="tpu_custom_call", output_to_operand_aliasing={{1}: (2, {})} | custom-call | flops 1 | bytes 1 | tf_op jit(solution)/shard_map/pallas_call | solution.py:33
  69.9 8.9 %collective-permute-start.11 = (bf16[512,128]{1,0:T(8,128)(2,1)}, bf16[512,128]{1,0:T(8,128)(2,1)}, u32[]{:S(2)}, u32[]{:S(2)}) collective-permute-start(bf16[512,128]{1,0:T(8,128)(2,1)} %get-tuple-element.58.refs_2_), channel_id=1, source_target_pairs={{0,1},{1,0},{2,3},{3,2},{4,5},{5,4},{6,7},{7,6},{8,9},{9,8},{10,11... | collective-permute-start | bytes 393224 | tf_op jit(solution)/shard_map/ppermute | solution.py:350
  78.9 9.9 %collective-permute-done.11.refs_3_ = bf16[512,128]{1,0:T(8,128)(2,1)} collective-permute-done((bf16[512,128]{1,0:T(8,128)(2,1)}, bf16[512,128]{1,0:T(8,128)(2,1)}, u32[]{:S(2)}, u32[]{:S(2)}) %collective-permute-start.11) | collective-permute-done | bytes 131104 | tf_op jit(solution)/shard_map/ppermute | solution.py:350
  88.7 7.8 %shard_map.85 = (f32[1024,512]{1,0:T(8,128)}, f32[8,128]{1,0:T(8,128)}) custom-call(bf16[1024,2048]{1,0:T(8,128)(2,1)} %refs_0_.7, bf16[2048,2048]{1,0:T(8,128)(2,1)} %refs_1_.7, bf16[512,128]{1,0:T(8,128)(2,1)} %get-tuple-element.58.refs_2_, bf16[512,128]{1,0:T(8,128)(2,1)} %collective-permute-done.11.refs_3_, ...), custom_call_target="tpu_custom_call", output_to_operand_aliasing={{1}: (9, {})} | custom-call | flops 1 | bytes 1 | tf_op jit(solution)/shard_map/pallas_call | solution.py:33
  96.6 3.4 %shard_map.86 = (f32[1024,512]{1,0:T(8,128)}, f32[8,128]{1,0:T(8,128)}) custom-call(f32[1024,512]{1,0:T(8,128)} %get-tuple-element.63.refs_0_, bf16[512,512]{1,0:T(8,128)(2,1)} %collective-permute-done.15.refs_1_, bf16[512,512]{1,0:T(8,128)(2,1)} %collective-permute-done.16.refs_2_, f32[8,128]{1,0:T(8,128)} %get-tuple-element.66.refs_3_), custom_call_target="tpu_custom_call", output_to_operand_aliasing={{1}: (3, {})} | custom-call | flops 1 | bytes 1 | tf_op jit(solution)/shard_map/pallas_call | solution.py:33
  99.9 3.0 %shard_map.87 = (bf16[1024,512]{1,0:T(8,128)(2,1)}, f32[8,128]{1,0:T(8,128)}) custom-call(f32[1024,512]{1,0:T(8,128)} %get-tuple-element.67.refs_0_, bf16[1024,512]{1,0:T(8,128)(2,1)} %collective-permute-done.17.refs_1_, f32[8,128]{1,0:T(8,128)} %get-tuple-element.69.refs_2_), custom_call_target="tpu_custom_call", output_to_operand_aliasing={{1}: (2, {})} | custom-call | flops 1 | bytes 1 | tf_op jit(solution)/shard_map/pallas_call | solution.py:33
  (36 shorter events, 9.1 us)
Async XLA Ops:
  3.9 15.5 %collective-permute-start.3 = (bf16[512,512]{1,0:T(8,128)(2,1)}, bf16[512,512]{1,0:T(8,128)(2,1)}, u32[]{:S(2)}, u32[]{:S(2)}) collective-permute-start(bf16[512,512]{1,0:T(8,128)(2,1)} %get-tuple-element.38.refs_0_), channel_id=1, source_target_pairs={{0,1},{1,0},{2,3},{3,2},{4,5},{5,4},{6,7},{7,6},{8,9},{9,8},{10,11... | collective-permute-start | bytes 1572872 | tf_op jit(solution)/shard_map/ppermute | solution.py:350
  7.0 16.5 %collective-permute-start.1 = (bf16[2048,128]{1,0:T(8,128)(2,1)}, bf16[2048,128]{1,0:T(8,128)(2,1)}, u32[]{:S(2)}, u32[]{:S(2)}) collective-permute-start(bf16[2048,128]{1,0:T(8,128)(2,1)} %refs_1_.6), channel_id=1, source_target_pairs={{0,8},{4,12},{8,0},{12,4},{1,9},{5,13},{9,1},{13,5},{2,10},{6,14},... | collective-permute-start | bytes 1572872 | tf_op jit(solution)/shard_map/ppermute | solution.py:356
  8.5 15.0 %collective-permute-start.2 = (bf16[128,512]{1,0:T(8,128)(2,1)}, bf16[128,512]{1,0:T(8,128)(2,1)}, u32[]{:S(2)}, u32[]{:S(2)}) collective-permute-start(bf16[128,512]{1,0:T(8,128)(2,1)} %refs_4_.1), channel_id=1, source_target_pairs={{0,8},{4,12},{8,0},{12,4},{1,9},{5,13},{9,1},{13,5},{2,10},{6,14},... | collective-permute-start | bytes 393224 | tf_op jit(solution)/shard_map/ppermute | solution.py:356
  9.0 19.2 %collective-permute-start = (bf16[2048,128]{1,0:T(8,128)(2,1)}, bf16[2048,128]{1,0:T(8,128)(2,1)}, u32[]{:S(2)}, u32[]{:S(2)}) collective-permute-start(bf16[2048,128]{1,0:T(8,128)(2,1)} %refs_1_.6), channel_id=1, source_target_pairs={{0,4},{4,0},{8,12},{12,8},{1,5},{5,1},{9,13},{13,9},{2,6},{6,2},{1... | collective-permute-start | bytes 1572872 | tf_op jit(solution)/shard_map/ppermute | solution.py:356
  9.0 16.6 %copy-start.1 = (s32[8]{0:T(128)S(1)}, s32[8]{0:T(128)}, u32[]{:S(2)}) copy-start(s32[8]{0:T(128)} %param.12) | copy-start | bytes 100
  9.0 16.6 %copy-start.2 = (s32[8]{0:T(128)S(1)}, s32[8]{0:T(128)}, u32[]{:S(2)}) copy-start(s32[8]{0:T(128)} %param.13) | copy-start | bytes 100
  9.0 16.6 %copy-start = (s32[1024,1]{0,1:T(1,128)S(1)}, s32[1024,1]{0,1:T(1,128)}, u32[]{:S(2)}) copy-start(s32[1024,1]{0,1:T(1,128)} %param.11) | copy-start | bytes 12292
  23.5 4.7 %collective-permute-start.4 = (bf16[2048,128]{1,0:T(8,128)(2,1)}, bf16[2048,128]{1,0:T(8,128)(2,1)}, u32[]{:S(2)}, u32[]{:S(2)}) collective-permute-start(bf16[2048,128]{1,0:T(8,128)(2,1)} %get-tuple-element.42.refs_3_), channel_id=1, source_target_pairs={{0,4},{4,0},{8,12},{12,8},{1,5},{5,1},{9,13},{13,9},{2,6},{6,2},{1... | collective-permute-start | bytes 1572872 | tf_op jit(solution)/shard_map/ppermute | solution.py:356
  23.5 15.1 %collective-permute-start.6 = (bf16[512,512]{1,0:T(8,128)(2,1)}, bf16[512,512]{1,0:T(8,128)(2,1)}, u32[]{:S(2)}, u32[]{:S(2)}) collective-permute-start(bf16[512,512]{1,0:T(8,128)(2,1)} %get-tuple-element.45.refs_0_), channel_id=1, source_target_pairs={{0,1},{1,0},{2,3},{3,2},{4,5},{5,4},{6,7},{7,6},{8,9},{9,8},{10,11... | collective-permute-start | bytes 1572872 | tf_op jit(solution)/shard_map/ppermute | solution.py:350
  23.9 30.4 %collective-permute-start.10 = (bf16[512,512]{1,0:T(8,128)(2,1)}, bf16[512,512]{1,0:T(8,128)(2,1)}, u32[]{:S(2)}, u32[]{:S(2)}) collective-permute-start(bf16[512,512]{1,0:T(8,128)(2,1)} %get-tuple-element.54.refs_0_), channel_id=1, source_target_pairs={{0,1},{1,0},{2,3},{3,2},{4,5},{5,4},{6,7},{7,6},{8,9},{9,8},{10,11... | collective-permute-start | bytes 1572872 | tf_op jit(solution)/shard_map/ppermute | solution.py:350
  26.8 29.7 %collective-permute-start.8 = (bf16[512,512]{1,0:T(8,128)(2,1)}, bf16[512,512]{1,0:T(8,128)(2,1)}, u32[]{:S(2)}, u32[]{:S(2)}) collective-permute-start(bf16[512,512]{1,0:T(8,128)(2,1)} %get-tuple-element.52), channel_id=1, source_target_pairs={{1,2},{2,1},{5,6},{6,5},{9,10},{10,9},{13,14},{14,13},{17,18},{18,... | collective-permute-start | bytes 1572872 | tf_op jit(solution)/shard_map/ppermute | solution.py:353
  40.8 15.7 %collective-permute-start.9 = (bf16[512,512]{1,0:T(8,128)(2,1)}, bf16[512,512]{1,0:T(8,128)(2,1)}, u32[]{:S(2)}, u32[]{:S(2)}) collective-permute-start(bf16[512,512]{1,0:T(8,128)(2,1)} %get-tuple-element.53), channel_id=1, source_target_pairs={{1,2},{2,1},{5,6},{6,5},{9,10},{10,9},{13,14},{14,13},{17,18},{18,... | collective-permute-start | bytes 1572872 | tf_op jit(solution)/shard_map/ppermute | solution.py:353
  42.2 10.5 %collective-permute-start.5 = (bf16[512,128]{1,0:T(8,128)(2,1)}, bf16[512,128]{1,0:T(8,128)(2,1)}, u32[]{:S(2)}, u32[]{:S(2)}) collective-permute-start(bf16[512,128]{1,0:T(8,128)(2,1)} %get-tuple-element.44.refs_0_), channel_id=1, source_target_pairs={{0,1},{1,0},{2,3},{3,2},{4,5},{5,4},{6,7},{7,6},{8,9},{9,8},{10,11... | collective-permute-start | bytes 393224 | tf_op jit(solution)/shard_map/ppermute | solution.py:350
  45.9 18.8 %collective-permute-start.14 = (bf16[512,512]{1,0:T(8,128)(2,1)}, bf16[512,512]{1,0:T(8,128)(2,1)}, u32[]{:S(2)}, u32[]{:S(2)}) collective-permute-start(bf16[512,512]{1,0:T(8,128)(2,1)} %get-tuple-element.60.refs_0_), channel_id=1, source_target_pairs={{0,1},{1,0},{2,3},{3,2},{4,5},{5,4},{6,7},{7,6},{8,9},{9,8},{10,11... | collective-permute-start | bytes 1572872 | tf_op jit(solution)/shard_map/ppermute | solution.py:350
  59.3 40.6 %collective-permute-start.17 = (bf16[1024,512]{1,0:T(8,128)(2,1)}, bf16[1024,512]{1,0:T(8,128)(2,1)}, u32[]{:S(2)}, u32[]{:S(2)}) collective-permute-start(bf16[1024,512]{1,0:T(8,128)(2,1)} %get-tuple-element.68), channel_id=1, source_target_pairs={{0,1},{1,0},{2,3},{3,2},{4,5},{5,4},{6,7},{7,6},{8,9},{9,8},{10,11... | collective-permute-start | bytes 3145736 | tf_op jit(solution)/shard_map/ppermute | solution.py:350
  60.3 2.8 %collective-permute-start.7 = (bf16[512,128]{1,0:T(8,128)(2,1)}, bf16[512,128]{1,0:T(8,128)(2,1)}, u32[]{:S(2)}, u32[]{:S(2)}) collective-permute-start(bf16[512,128]{1,0:T(8,128)(2,1)} %get-tuple-element.50.refs_0_), channel_id=1, source_target_pairs={{1,2},{2,1},{5,6},{6,5},{9,10},{10,9},{13,14},{14,13},{17,18},{18,... | collective-permute-start | bytes 393224 | tf_op jit(solution)/shard_map/ppermute | solution.py:353
  61.6 35.0 %collective-permute-start.15 = (bf16[512,512]{1,0:T(8,128)(2,1)}, bf16[512,512]{1,0:T(8,128)(2,1)}, u32[]{:S(2)}, u32[]{:S(2)}) collective-permute-start(bf16[512,512]{1,0:T(8,128)(2,1)} %get-tuple-element.64), channel_id=1, source_target_pairs={{1,2},{2,1},{5,6},{6,5},{9,10},{10,9},{13,14},{14,13},{17,18},{18,... | collective-permute-start | bytes 1572872 | tf_op jit(solution)/shard_map/ppermute | solution.py:353
  66.8 29.8 %collective-permute-start.16 = (bf16[512,512]{1,0:T(8,128)(2,1)}, bf16[512,512]{1,0:T(8,128)(2,1)}, u32[]{:S(2)}, u32[]{:S(2)}) collective-permute-start(bf16[512,512]{1,0:T(8,128)(2,1)} %get-tuple-element.65), channel_id=1, source_target_pairs={{1,2},{2,1},{5,6},{6,5},{9,10},{10,9},{13,14},{14,13},{17,18},{18,... | collective-permute-start | bytes 1572872 | tf_op jit(solution)/shard_map/ppermute | solution.py:353
  68.2 1.7 %collective-permute-start.12 = (bf16[128,512]{1,0:T(8,128)(2,1)}, bf16[128,512]{1,0:T(8,128)(2,1)}, u32[]{:S(2)}, u32[]{:S(2)}) collective-permute-start(bf16[128,512]{1,0:T(8,128)(2,1)} %refs_4_.1), channel_id=1, source_target_pairs={{0,4},{4,0},{8,12},{12,8},{1,5},{5,1},{9,13},{13,9},{2,6},{6,2},{1... | collective-permute-start | bytes 393224 | tf_op jit(solution)/shard_map/ppermute | solution.py:356
  68.2 10.6 %collective-permute-start.13 = (bf16[128,512]{1,0:T(8,128)(2,1)}, bf16[128,512]{1,0:T(8,128)(2,1)}, u32[]{:S(2)}, u32[]{:S(2)}) collective-permute-start(bf16[128,512]{1,0:T(8,128)(2,1)} %get-tuple-element.59.refs_6_), channel_id=1, source_target_pairs={{0,4},{4,0},{8,12},{12,8},{1,5},{5,1},{9,13},{13,9},{2,6},{6,2},{1... | collective-permute-start | bytes 393224 | tf_op jit(solution)/shard_map/ppermute | solution.py:356
  69.9 18.8 %collective-permute-start.11 = (bf16[512,128]{1,0:T(8,128)(2,1)}, bf16[512,128]{1,0:T(8,128)(2,1)}, u32[]{:S(2)}, u32[]{:S(2)}) collective-permute-start(bf16[512,128]{1,0:T(8,128)(2,1)} %get-tuple-element.58.refs_2_), channel_id=1, source_target_pairs={{0,1},{1,0},{2,3},{3,2},{4,5},{5,4},{6,7},{7,6},{8,9},{9,8},{10,11... | collective-permute-start | bytes 393224 | tf_op jit(solution)/shard_map/ppermute | solution.py:350

commit v3 on v2

v3 whole, which is shorter than its diff:
```python
import functools

import jax
import jax.numpy as jnp
from jax import lax
from jax.experimental import pallas as pl
from jax.experimental.pallas import tpu as pltpu
from jax.sharding import PartitionSpec as P

F32 = jnp.float32
BF16 = jnp.bfloat16
LANES = 128
PIECES = 4
ANY = pl.BlockSpec(memory_space=pl.ANY)
VMEM = pl.BlockSpec(memory_space=pltpu.VMEM)
PARAMS = pltpu.CompilerParams(vmem_limit_bytes=64 * 1024 * 1024 - 128 * 1024)
COST = pl.CostEstimate(flops=1, bytes_accessed=1, transcendentals=0)


def call(kernel, outs, in_specs, scratch, token, *args, out_specs, aliases=None):
    n_in, n_out = len(args), len(outs)
    aliases = dict(aliases or {})
    if token is not None:
        args += (token,)
        in_specs = [*in_specs, ANY]
        aliases[n_in] = n_out

    def body(*refs):
        given = refs[:n_in]
        rest = refs[len(args) :]
        kernel(*given, *rest[:n_out], *rest[n_out + 1 :])

    return pl.pallas_call(
        body,
        out_shape=(*outs, jax.ShapeDtypeStruct((8, LANES), F32)),
        in_specs=in_specs,
        out_specs=(*out_specs, ANY),
        scratch_shapes=scratch,
        input_output_aliases=aliases,
        compiler_params=PARAMS,
        cost_estimate=COST,
    )(*args)


def relay(token, *arrays):
    return call(
        lambda *refs: None,
        [jax.ShapeDtypeStruct(a.shape, a.dtype) for a in arrays],
        [ANY] * len(arrays),
        [],
        token,
        *arrays,
        out_specs=[ANY] * len(arrays),
        aliases={i: i for i in range(len(arrays))},
    )


def in_middle():
    me = lax.axis_index("tensor")
    return jnp.logical_and(me > 0, me < 3)


def block_of(phase):
    me = lax.axis_index("tensor")
    if phase == 0:
        return jnp.where(me < 2, 3, 0)
    if phase == 1:
        return jnp.where(me < 2, 2, 1)
    if phase == 2:
        return me + 1 - 2 * lax.rem(me, 2)
    return me


def copy_in(pairs, sems):
    copies = [pltpu.make_async_copy(a, b, sems.at[i]) for i, (a, b) in enumerate(pairs)]
    for c in copies:
        c.start()
    return copies


def fetch(hidden, weight, lo, rows, phase, first_row, h_buf, w_buf, h_sem, w_sem):
    depth, cols = w_buf.shape
    step = depth // PIECES
    first = pl.multiple_of(block_of(phase) * cols, cols)
    h_copies, w_copies = [], []
    for k in range(PIECES):
        span = pl.ds(k * step, step)
        if h_sem is not None:
            pair = (hidden.at[pl.ds(lo, rows), span], h_buf.at[pl.ds(lo - first_row, rows), span])
            h_copies += copy_in([pair], h_sem.at[pl.ds(k, 1)])
        pair = (weight.at[span, pl.ds(first, cols)], w_buf.at[span])
        w_copies += copy_in([pair], w_sem.at[pl.ds(k, 1)])
    return h_copies, w_copies


def product(h_buf, w_buf, lo, rows, copies):
    h_copies, w_copies = copies
    step = w_buf.shape[0] // PIECES
    total = None
    for k in range(PIECES):
        if h_copies:
            h_copies[k].wait()
        if w_copies:
            w_copies[k].wait()
        span = pl.ds(k * step, step)
        term = jnp.dot(h_buf[pl.ds(lo, rows), span], w_buf[span], preferred_element_type=F32)
        total = term if total is None else total + term
    return total


def products_kernel(jobs, count, hidden, weight, *rest):
    outs, (h_buf, w_buf, buf, h_sem, w_sem, o_sem) = rest[:count], rest[count:]
    first = min(job[1] for job in jobs)
    copies, loaded = [], set()
    for j, (phase, lo, rows, _, _) in enumerate(jobs):
        fresh = not set(range(lo, lo + rows)) <= loaded
        loaded |= set(range(lo, lo + rows))
        sems = h_sem.at[j] if fresh else None
        copies.append(fetch(hidden, weight, lo, rows, phase, first, h_buf, w_buf.at[j], sems, w_sem.at[j]))
    sent = []
    for j, (_, lo, rows, o, at) in enumerate(jobs):
        value = product(h_buf, w_buf.at[j], lo - first, rows, copies[j])
        buf[j, pl.ds(0, rows)] = value.astype(BF16)
        pair = (buf.at[j, pl.ds(0, rows)], outs[o].at[pl.ds(at, rows)])
        sent += copy_in([pair], o_sem.at[pl.ds(j, 1)])
    for c in sent:
        c.wait()


def products(token, hidden, weight, jobs, heights):
    depth = hidden.shape[1]
    cols = weight.shape[1] // 4
    first = min(job[1] for job in jobs)
    last = max(job[1] + job[2] for job in jobs)
    most = max(job[2] for job in jobs)
    count = len(jobs)
    return call(
        functools.partial(products_kernel, jobs, len(heights)),
        [jax.ShapeDtypeStruct((rows, cols), BF16) for rows in heights],
        [ANY] * 2,
        [
            pltpu.VMEM((last - first, depth), BF16),
            pltpu.VMEM((count, depth, cols), BF16),
            pltpu.VMEM((count, most, cols), BF16),
            pltpu.SemaphoreType.DMA((count, PIECES)),
            pltpu.SemaphoreType.DMA((count, PIECES)),
            pltpu.SemaphoreType.DMA((count,)),
        ],
        token,
        hidden,
        weight,
        out_specs=[ANY] * len(heights),
    )


def add_kernel(a, b, *outs):
    at = 0
    for out in outs:
        rows = pl.ds(at, out.shape[0])
        out[...] = (a[rows].astype(F32) + b[rows].astype(F32)).astype(BF16)
        at += out.shape[0]


def add(token, a, b, heights=None):
    outs = [jax.ShapeDtypeStruct((rows, a.shape[1]), BF16) for rows in heights or (a.shape[0],)]
    return call(add_kernel, outs, [VMEM, VMEM], [], token, a, b, out_specs=[VMEM] * len(outs))


def add_middle_kernel(lo, spans, p, *rest):
    count = len(spans)
    givens, (out, p_buf, g_buf, sem) = rest[:count], rest[count:]
    pairs, to = [(p.at[pl.ds(lo, out.shape[0])], p_buf)], 0
    for g, (at, rows) in zip(givens, spans):
        pairs.append((g.at[pl.ds(at, rows)], g_buf.at[pl.ds(to, rows)]))
        to += rows
    for c in copy_in(pairs, sem):
        c.wait()
    other = jnp.where(in_middle(), g_buf[...].astype(F32), 0.0)
    out[...] = (p_buf[...].astype(F32) + other).astype(BF16)


def add_middle(token, p, lo, givens, spans):
    shape = (sum(rows for _, rows in spans), p.shape[1])
    return call(
        functools.partial(add_middle_kernel, lo, spans),
        [jax.ShapeDtypeStruct(shape, BF16)],
        [ANY] * (1 + len(givens)),
        [pltpu.VMEM(shape, BF16)] * 2 + [pltpu.SemaphoreType.DMA((1 + len(givens),))],
        token,
        p,
        *givens,
        out_specs=[VMEM],
    )


def low_kernel(hidden, y0, y1, y2, y3, code, _, out, h_buf, w_buf, acc, low, h_sem, w_sem, o_sem):
    rows, depth = hidden.shape
    step = depth // PIECES
    h_copies, w_copies = [], []
    for k in range(PIECES):
        span = pl.ds(k * step, step)
        h_copies += copy_in([(hidden.at[:, span], h_buf.at[:, span])], h_sem.at[pl.ds(k, 1)])
        for p, y in enumerate((y0, y1, y2, y3)):
            pair = (y.at[span], w_buf.at[span, pl.ds(p * LANES, LANES)])
            w_copies += copy_in([pair], w_sem.at[pl.ds(4 * k + p, 1)])
    for k in range(PIECES):
        h_copies[k].wait()
        for p in range(4):
            w_copies[4 * k + p].wait()
        span = pl.ds(k * step, step)
        product = jnp.dot(h_buf[:, span], w_buf[span], preferred_element_type=F32)
        if k == 0:
            acc[...] = product
        else:
            acc[...] += product
    width = LANES // 2
    tile = rows // 8
    owner = lax.broadcasted_iota(jnp.int32, (tile, 4 * LANES), 1) // width
    lane = lax.broadcasted_iota(jnp.int32, (tile, LANES), 1)

    def own_columns(at):
        mine = jnp.where(owner == code[at] // LANES, acc[at], 0.0)
        both = mine[:, :LANES]
        for p in range(1, 4):
            both = both + mine[:, p * LANES : (p + 1) * LANES]
        return both + pltpu.roll(both, width, 1)

    for t in range(4):
        first, second = own_columns(pl.ds(2 * t * tile, tile)), own_columns(pl.ds((2 * t + 1) * tile, tile))
        low[:, pl.ds(t * LANES, LANES)] = jnp.where(lane < width, first, second).astype(BF16)
    for c in copy_in([(low, out.at[pl.ds(out.shape[0] - tile, tile)])], o_sem):
        c.wait()


def low_product(token, hidden, ys, code, under):
    rows, depth = hidden.shape
    return call(
        low_kernel,
        [jax.ShapeDtypeStruct(under.shape, BF16)],
        [ANY] * 5 + [VMEM, ANY],
        [
            pltpu.VMEM((rows, depth), BF16),
            pltpu.VMEM((depth, 4 * LANES), BF16),
            pltpu.VMEM((rows, 4 * LANES), F32),
            pltpu.VMEM((rows // 8, 4 * LANES), BF16),
            pltpu.SemaphoreType.DMA((PIECES,)),
            pltpu.SemaphoreType.DMA((4 * PIECES,)),
            pltpu.SemaphoreType.DMA((1,)),
        ],
        token,
        hidden,
        *ys,
        code,
        under,
        out_specs=[ANY],
        aliases={6: 0},
    )


def own_kernel(hidden, weight, out, h_buf, w_buf, h_sem, w_sem):
    rows = hidden.shape[0]
    copies = fetch(hidden, weight, 0, rows, 3, 0, h_buf, w_buf, h_sem, w_sem)
    out[...] = product(h_buf, w_buf, 0, rows, copies)


def own_product(token, hidden, weight):
    rows, depth = hidden.shape
    cols = weight.shape[1] // 4
    return call(
        own_kernel,
        [jax.ShapeDtypeStruct((rows, cols), F32)],
        [ANY] * 2,
        [
            pltpu.VMEM((rows, depth), BF16),
            pltpu.VMEM((depth, cols), BF16),
            pltpu.SemaphoreType.DMA((PIECES,)),
            pltpu.SemaphoreType.DMA((PIECES,)),
        ],
        token,
        hidden,
        weight,
        out_specs=[VMEM],
    )


def up_kernel(own, low, other, y0, y1, y2, y3, code, b, m, out, rest, u_buf, sem):
    rows, cols = own.shape
    ups = copy_in([(y, u_buf.at[pl.ds(p * LANES, LANES)]) for p, y in enumerate((y0, y1, y2, y3))], sem)
    for c in ups:
        c.wait()
    middle = in_middle()
    width = LANES // 2
    half = rows // 2
    tile = rows // 8
    column = lax.broadcasted_iota(jnp.int32, (tile, 4 * LANES), 1) // width
    lane = lax.broadcasted_iota(jnp.int32, (tile, LANES), 1)
    b_at = b.shape[0] - half
    for t in range(4):
        lanes = pl.ds(t * LANES, LANES)
        pair = low[:, lanes].astype(F32) + other[:, lanes].astype(F32)
        turned = pltpu.roll(pair, width, 1)
        spreads = []
        for k in range(2):
            rows_at = pl.ds((2 * t + k) * tile, tile)
            mine = jnp.where(lane < width, turned, pair) if k else jnp.where(lane < width, pair, turned)
            live = lax.rem(code[rows_at], LANES)
            mine = mine * (width / (2.0 * live.astype(F32)))
            mine = jnp.where(lax.rem(lane, width) < live, mine, 0.0)
            spread = jnp.concatenate([mine] * 4, axis=1)
            spreads.append(jnp.where(column == code[rows_at] // LANES, spread, 0.0).astype(BF16))
        at = pl.ds(2 * t * tile, 2 * tile)
        spread = jnp.concatenate(spreads, axis=0)
        total = own[at] + jnp.dot(spread, u_buf[...], preferred_element_type=F32)
        if t < 2:
            inner = b[pl.ds(b_at + 2 * t * tile, 2 * tile)].astype(F32)
            total = total + jnp.where(middle, inner, 0.0)
            out[at] = (total + m[at].astype(F32)).astype(BF16)
        else:
            rest[pl.ds((2 * t - 4) * tile, 2 * tile)] = total


def up_sum(token, own, low, other, ys, code, b, m):
    rows, cols = own.shape
    return call(
        up_kernel,
        [jax.ShapeDtypeStruct((rows, cols), BF16), jax.ShapeDtypeStruct((rows // 2, cols), F32)],
        [VMEM] * 3 + [ANY] * 4 + [VMEM] * 3,
        [
            pltpu.VMEM((4 * LANES, cols), BF16),
            pltpu.SemaphoreType.DMA((4,)),
        ],
        token,
        own,
        low,
        other,
        *ys,
        code,
        b,
        m,
        out_specs=[VMEM] * 2,
    )


def last_kernel(done, rest, b, m, out, buf, sem):
    half = rest.shape[0]
    total = rest[...] + jnp.where(in_middle(), b[...].astype(F32), 0.0)
    buf[...] = (total + m[...].astype(F32)).astype(BF16)
    for c in copy_in([(buf, out.at[pl.ds(half, half)])], sem):
        c.wait()


def last_sum(token, done, rest, b, m):
    return call(
        last_kernel,
        [jax.ShapeDtypeStruct(done.shape, BF16)],
        [ANY] + [VMEM] * 3,
        [pltpu.VMEM(rest.shape, BF16), pltpu.SemaphoreType.DMA((1,))],
        token,
        done,
        rest,
        b,
        m,
        out_specs=[ANY],
        aliases={0: 0},
    )[0]


def by_adapter(row_adapter, values):
    every = jnp.arange(values.shape[0], dtype=jnp.int32)
    return jnp.sum(jnp.where(row_adapter == every[None, :], values[None, :], 0), axis=1, keepdims=True)


def line_of_four(hidden, weight, down, up, row_adapter, rank_of_adapter, adapter_storage_slot):
    rows = hidden.shape[0]
    half = rows // 2
    at = lax.axis_index("dp")
    per_index = adapter_storage_slot.shape[0] // 4

    def send(v, pairs):
        return lax.ppermute(v, "tensor", pairs)

    near = [(0, 1), (1, 0), (2, 3), (3, 2)]
    middle = [(1, 2), (2, 1)]
    two = [(0, 2), (2, 0), (1, 3), (3, 1)]

    def swap(v, bit):
        return lax.ppermute(v, "dp", [(i, i ^ bit) for i in range(4)])

    places = ((adapter_storage_slot // per_index) ^ at) * per_index + adapter_storage_slot % per_index
    code = by_adapter(row_adapter, places * LANES + rank_of_adapter)

    down2, down1 = swap(down, 2), swap(down, 1)
    up2, up1 = swap(up, 2), swap(up, 1)

    cut = rows * 3 // 4
    after = rows - cut
    p0a, t = products(None, hidden, weight, [(0, 0, cut, 0, 0)], [cut])
    a1a = send(p0a, near)
    jobs = [(1, 0, half, 0, after), (1, half, half, 1, 0), (0, cut, after, 0, 0), (2, 0, rows, 2, 0)]
    p01, p1l, p2, t = products(t, hidden, weight, jobs, [after + half, half + rows // 8, rows])
    a12 = send(p01, near)
    down2, t = relay(t, down2)
    downs = (down, down1, down2, swap(down2, 1))
    v, t = add(t, p0a, a1a)
    b1a = send(v, middle)
    p1l, t = low_product(t, hidden, downs, code, p1l)
    a2l = send(p1l, near)
    v, t = add(t, p01, a12)
    b12 = send(v, middle)
    v, t = add_middle(t, p2, 0, (b1a,), [(0, half)])
    m3a = send(v, near)
    own, t = own_product(t, hidden, weight)
    up2, t = relay(t, up2)
    ups = (up, up1, up2, swap(up2, 1))
    v, low, t = add(t, p1l, a2l, [half, rows // 8])
    b2b = send(v, middle)
    e2 = send(low, two)
    m, t = add_middle(t, p2, half, (b1a, b12), [(half, cut - half), (0, after)])
    m, m3a, e2, t = relay(t, m, m3a, e2)
    m3b = send(m, near)
    out, rest, t = up_sum(t, own, low, e2, ups, code, b12, m3a)
    return last_sum(t, out, rest, b2b, m3b)


def any_line(hidden, weight, down, up, row_adapter, rank_of_adapter, adapter_storage_slot):
    rows = hidden.shape[0]
    adapters = rank_of_adapter.shape[0]
    width = down.shape[1] * lax.axis_size("dp") // adapters
    slot = by_adapter(row_adapter, adapter_storage_slot)
    rank = by_adapter(row_adapter, rank_of_adapter)
    chosen = slot == jnp.arange(adapters, dtype=jnp.int32)[None, :]
    partial = jnp.dot(hidden, weight, preferred_element_type=F32).astype(BF16)
    base = lax.psum_scatter(partial, "tensor", scatter_dimension=1, tiled=True).astype(F32)
    downs = lax.all_gather(down, "dp", axis=1, tiled=True)
    product = jnp.dot(hidden, downs, preferred_element_type=F32)
    low = jnp.einsum("rac,ra->rc", product.reshape(rows, adapters, width), chosen.astype(F32))
    low = lax.psum(low.astype(BF16), "tensor").astype(F32)
    live = jnp.arange(width, dtype=jnp.int32)[None, :] < rank
    scaling = width / (2.0 * rank.astype(F32))
    low_rank = jnp.where(live, low * scaling, F32(0.0)).astype(BF16)
    spread = jnp.where(chosen[:, :, None], low_rank[:, None, :], jnp.zeros((), BF16)).reshape(rows, -1)
    ups = lax.all_gather(up, "dp", axis=0, tiled=True)
    return (base + jnp.dot(spread, ups, preferred_element_type=F32)).astype(BF16)


def on_device(hidden, weight, down, up, *rest):
    fits = (
        lax.axis_size("tensor") == 4
        and lax.axis_size("dp") == 4
        and down.shape[1] == LANES
        and up.shape[0] == LANES
        and rest[1].shape[0] == 8
        and hidden.shape[0] % 1024 == 0
        and hidden.shape[1] % (PIECES * LANES) == 0
        and up.shape[1] == 4 * LANES
    )
    return (line_of_four if fits else any_line)(hidden, weight, down, up, *rest)


def solution(mesh):
    return jax.shard_map(
        on_device,
        mesh=mesh,
        in_specs=(
            P(("groups", "dp"), "tensor"),
            P("tensor", None),
            P("tensor", "dp"),
            P("dp", "tensor"),
            P(("groups", "dp"), None),
            P(),
            P(),
        ),
        out_specs=P(("groups", "dp"), "tensor"),
        check_vma=False,
    )
```

time: 103 us -> 88.5 us (0.86)
  starting transfers between devices: 28.5 us -> 20.5 us
  waiting for transfers between devices: 23.8 us -> 19.7 us
  Pallas kernels: 49.4 us -> 46.6 us
    ppermute x12 -> x9, starting transfers between devices: 25.9 us -> 17 us  [send(): return lax.ppermute(v, 'tensor', pairs)]
    ppermute x12 -> x9, waiting for transfers between devices: 20.6 us -> 17 us  [send(): return lax.ppermute(v, 'tensor', pairs)]
    pallas_call x15 -> x14, Pallas kernels: 49.4 us -> 46.6 us  [call(): pl.pallas_call(body, out_shape=(*outs, jax.ShapeDtypeStruct((8, LANES), F...]
  transfers between devices with their start and end apart: 18 -> 15, of which waited for: 5 -> 7; matrix products, arithmetic and copies ran while one was open for 1% -> 1% of each run, Pallas kernels for 41% -> 45%
where the time goes in v3:
time: 88.5 us; the launch traced here: 88.1 us
  Pallas kernels  46.6 us (53%)
  starting transfers between devices  20.5 us (23%)
  waiting for transfers between devices  19.7 us (22%)
  local copies, waits for them, and re-layouts  1.07 us (1%)
    pallas_call x14, Pallas kernels, call(): pl.pallas_call(body, out_shape=(*outs, jax.ShapeDtypeStruct((8, LANES), F...  46.6 us
    ppermute x9, starting transfers between devices, send(): return lax.ppermute(v, 'tensor', pairs)  17 us
    ppermute x9, waiting for transfers between devices, send(): return lax.ppermute(v, 'tensor', pairs)  17 us
    ppermute x6, starting transfers between devices, swap(): return lax.ppermute(v, 'dp', [(i, i ^ bit) for i in range(4)])  3.5 us
    ppermute x6, waiting for transfers between devices, swap(): return lax.ppermute(v, 'dp', [(i, i ^ bit) for i in range(4)])  2.76 us
  transfers between devices with their start and end apart: 15, of which 7 were waited for; matrix products, arithmetic and copies ran while one was open for 1% of the time, Pallas kernels for 45%

profile of v3, /device:TPU:0, one launch (start us, length us, event | category | flops | bytes accessed | tf_op | source)
XLA Modules:
  0.0 88.1 jit_solution(10808371593475757272)
XLA Ops:
  0.0 4.8 %shard_map.73 = (bf16[768,512]{1,0:T(8,128)(2,1)}, f32[8,128]{1,0:T(8,128)}) custom-call(bf16[1024,2048]{1,0:T(8,128)(2,1)} %refs_0_.7, bf16[2048,2048]{1,0:T(8,128)(2,1)} %refs_1_.7), custom_call_target="tpu_custom_call" | custom-call | flops 1 | bytes 1 | tf_op jit(solution)/shard_map/pallas_call | solution.py:33
  4.8 3.1 %collective-permute-start = (bf16[768,512]{1,0:T(8,128)(2,1)}, bf16[768,512]{1,0:T(8,128)(2,1)}, u32[]{:S(2)}, u32[]{:S(2)}) collective-permute-start(bf16[768,512]{1,0:T(8,128)(2,1)} %get-tuple-element.40.refs_0_), channel_id=1, source_target_pairs={{0,1},{1,0},{2,3},{3,2},{4,5},{5,4},{6,7},{7,6},{8,9},{9,8},{10,11... | collective-permute-start | bytes 2359304 | tf_op jit(solution)/shard_map/ppermute | solution.py:380
  7.9 1.5 %collective-permute-start.1 = (bf16[2048,128]{1,0:T(8,128)(2,1)}, bf16[2048,128]{1,0:T(8,128)(2,1)}, u32[]{:S(2)}, u32[]{:S(2)}) collective-permute-start(bf16[2048,128]{1,0:T(8,128)(2,1)} %refs_1_.6), channel_id=1, source_target_pairs={{0,8},{4,12},{8,0},{12,4},{1,9},{5,13},{9,1},{13,5},{2,10},{6,14},... | collective-permute-start | bytes 1572872 | tf_op jit(solution)/shard_map/ppermute | solution.py:387
  9.4 10.3 %shard_map.74 = (bf16[768,512]{1,0:T(8,128)(2,1)}, bf16[640,512]{1,0:T(8,128)(2,1)}, bf16[1024,512]{1,0:T(8,128)(2,1)}, f32[8,128]{1,0:T(8,128)}) custom-call(bf16[1024,2048]{1,0:T(8,128)(2,1)} %refs_0_.7, bf16[2048,2048]{1,0:T(8,128)(2,1)} %refs_1_.7, f32[8,128]{1,0:T(8,128)} %get-tuple-element.38.refs_2_), custom_call_target="tpu_custom_call", output_to_operand_aliasing={{3}: (2, {})} | custom-call | flops 1 | bytes 1 | tf_op jit(solution)/shard_map/pallas_call | solution.py:33
  20.2 1.4 %collective-permute-done.1.refs_0_ = bf16[2048,128]{1,0:T(8,128)(2,1)} collective-permute-done((bf16[2048,128]{1,0:T(8,128)(2,1)}, bf16[2048,128]{1,0:T(8,128)(2,1)}, u32[]{:S(2)}, u32[]{:S(2)}) %collective-permute-start.1) | collective-permute-done | bytes 524320 | tf_op jit(solution)/shard_map/ppermute | solution.py:387
  21.6 5.0 %collective-permute-done.refs_1_ = bf16[768,512]{1,0:T(8,128)(2,1)} collective-permute-done((bf16[768,512]{1,0:T(8,128)(2,1)}, bf16[768,512]{1,0:T(8,128)(2,1)}, u32[]{:S(2)}, u32[]{:S(2)}) %collective-permute-start) | collective-permute-done | bytes 786464 | tf_op jit(solution)/shard_map/ppermute | solution.py:380
  26.6 2.4 %shard_map.76 = (bf16[768,512]{1,0:T(8,128)(2,1)}, f32[8,128]{1,0:T(8,128)}) custom-call(bf16[768,512]{1,0:T(8,128)(2,1)} %get-tuple-element.40.refs_0_, bf16[768,512]{1,0:T(8,128)(2,1)} %collective-permute-done.refs_1_, f32[8,128]{1,0:T(8,128)} %get-tuple-element.42.refs_2_), custom_call_target="tpu_custom_call", output_to_operand_aliasing={{1}: (2, {})} | custom-call | flops 1 | bytes 1 | tf_op jit(solution)/shard_map/pallas_call | solution.py:33
  29.0 1.5 %collective-permute-start.2 = (bf16[768,512]{1,0:T(8,128)(2,1)}, bf16[768,512]{1,0:T(8,128)(2,1)}, u32[]{:S(2)}, u32[]{:S(2)}) collective-permute-start(bf16[768,512]{1,0:T(8,128)(2,1)} %get-tuple-element.43), channel_id=1, source_target_pairs={{1,2},{2,1},{5,6},{6,5},{9,10},{10,9},{13,14},{14,13},{17,18},{18,... | collective-permute-start | bytes 2359304 | tf_op jit(solution)/shard_map/ppermute | solution.py:380
  31.7 6.4 %shard_map.77 = (bf16[640,512]{1,0:T(8,128)(2,1)}, f32[8,128]{1,0:T(8,128)}) custom-call(bf16[1024,2048]{1,0:T(8,128)(2,1)} %refs_0_.7, bf16[2048,128]{1,0:T(8,128)(2,1)} %refs_1_.6, bf16[2048,128]{1,0:T(8,128)(2,1)} %collective-permute-done.4.refs_2_, bf16[2048,128]{1,0:T(8,128)(2,1)} %get-tuple-element.45.refs_3_, ...), custom_call_target="tpu_custom_call", output_to_operand_aliasing={{0}: (6, {}), {1}: (7, {})} | custom-call | flops 1 | bytes 1 | tf_op jit(solution)/shard_map/pallas_call | solution.py:33
  38.1 4.1 %collective-permute-start.6 = (bf16[640,512]{1,0:T(8,128)(2,1)}, bf16[640,512]{1,0:T(8,128)(2,1)}, u32[]{:S(2)}, u32[]{:S(2)}) collective-permute-start(bf16[640,512]{1,0:T(8,128)(2,1)} %get-tuple-element.52.refs_0_), channel_id=1, source_target_pairs={{0,1},{1,0},{2,3},{3,2},{4,5},{5,4},{6,7},{7,6},{8,9},{9,8},{10,11... | collective-permute-start | bytes 1966088 | tf_op jit(solution)/shard_map/ppermute | solution.py:380
  42.2 1.2 %collective-permute-done.3.refs_1_ = bf16[768,512]{1,0:T(8,128)(2,1)} collective-permute-done((bf16[768,512]{1,0:T(8,128)(2,1)}, bf16[768,512]{1,0:T(8,128)(2,1)}, u32[]{:S(2)}, u32[]{:S(2)}) %collective-permute-start.3) | collective-permute-done | bytes 786464 | tf_op jit(solution)/shard_map/ppermute | solution.py:380
  43.4 2.5 %shard_map.78 = (bf16[768,512]{1,0:T(8,128)(2,1)}, f32[8,128]{1,0:T(8,128)}) custom-call(bf16[768,512]{1,0:T(8,128)(2,1)} %get-tuple-element.44.refs_0_, bf16[768,512]{1,0:T(8,128)(2,1)} %collective-permute-done.3.refs_1_, f32[8,128]{1,0:T(8,128)} %get-tuple-element.48.refs_2_), custom_call_target="tpu_custom_call", output_to_operand_aliasing={{1}: (2, {})} | custom-call | flops 1 | bytes 1 | tf_op jit(solution)/shard_map/pallas_call | solution.py:33
  45.9 1.5 %collective-permute-start.8 = (bf16[768,512]{1,0:T(8,128)(2,1)}, bf16[768,512]{1,0:T(8,128)(2,1)}, u32[]{:S(2)}, u32[]{:S(2)}) collective-permute-start(bf16[768,512]{1,0:T(8,128)(2,1)} %get-tuple-element.56), channel_id=1, source_target_pairs={{1,2},{2,1},{5,6},{6,5},{9,10},{10,9},{13,14},{14,13},{17,18},{18,... | collective-permute-start | bytes 2359304 | tf_op jit(solution)/shard_map/ppermute | solution.py:380
  47.4 2.2 %shard_map.79 = (bf16[512,512]{1,0:T(8,128)(2,1)}, f32[8,128]{1,0:T(8,128)}) custom-call(bf16[1024,512]{1,0:T(8,128)(2,1)} %get-tuple-element.39.refs_0_, bf16[768,512]{1,0:T(8,128)(2,1)} %collective-permute-done.2.refs_1_, f32[8,128]{1,0:T(8,128)} %get-tuple-element.49.refs_2_), custom_call_target="tpu_custom_call", output_to_operand_aliasing={{1}: (2, {})} | custom-call | flops 1 | bytes 1 | tf_op jit(solution)/shard_map/pallas_call | solution.py:33
  49.6 4.1 %collective-permute-start.9 = (bf16[512,512]{1,0:T(8,128)(2,1)}, bf16[512,512]{1,0:T(8,128)(2,1)}, u32[]{:S(2)}, u32[]{:S(2)}) collective-permute-start(bf16[512,512]{1,0:T(8,128)(2,1)} %get-tuple-element.59), channel_id=1, source_target_pairs={{0,1},{1,0},{2,3},{3,2},{4,5},{5,4},{6,7},{7,6},{8,9},{9,8},{10,11... | collective-permute-start | bytes 1572872 | tf_op jit(solution)/shard_map/ppermute | solution.py:380
  53.7 1.5 %collective-permute-start.7 = (bf16[128,512]{1,0:T(8,128)(2,1)}, bf16[128,512]{1,0:T(8,128)(2,1)}, u32[]{:S(2)}, u32[]{:S(2)}) collective-permute-start(bf16[128,512]{1,0:T(8,128)(2,1)} %refs_3_.1), channel_id=1, source_target_pairs={{0,8},{4,12},{8,0},{12,4},{1,9},{5,13},{9,1},{13,5},{2,10},{6,14},... | collective-permute-start | bytes 393224 | tf_op jit(solution)/shard_map/ppermute | solution.py:387
  55.2 5.7 %shard_map.80 = (f32[1024,512]{1,0:T(8,128)}, f32[8,128]{1,0:T(8,128)}) custom-call(bf16[1024,2048]{1,0:T(8,128)(2,1)} %refs_0_.7, bf16[2048,2048]{1,0:T(8,128)(2,1)} %refs_1_.7, f32[8,128]{1,0:T(8,128)} %get-tuple-element.50.refs_2_), custom_call_target="tpu_custom_call", output_to_operand_aliasing={{1}: (2, {})} | custom-call | flops 1 | bytes 1 | tf_op jit(solution)/shard_map/pallas_call | solution.py:33
  60.9 2.3 %shard_map.82 = (bf16[512,512]{1,0:T(8,128)(2,1)}, bf16[128,512]{1,0:T(8,128)(2,1)}, f32[8,128]{1,0:T(8,128)}) custom-call(bf16[640,512]{1,0:T(8,128)(2,1)} %get-tuple-element.52.refs_0_, bf16[640,512]{1,0:T(8,128)(2,1)} %collective-permute-done.6.refs_1_, f32[8,128]{1,0:T(8,128)} %get-tuple-element.54.refs_2_), custom_call_target="tpu_custom_call", output_to_operand_aliasing={{2}: (2, {})} | custom-call | flops 1 | bytes 1 | tf_op jit(solution)/shard_map/pallas_call | solution.py:33
  63.8 1.5 %collective-permute-start.13 = (bf16[512,512]{1,0:T(8,128)(2,1)}, bf16[512,512]{1,0:T(8,128)(2,1)}, u32[]{:S(2)}, u32[]{:S(2)}) collective-permute-start(bf16[512,512]{1,0:T(8,128)(2,1)} %get-tuple-element.67), channel_id=1, source_target_pairs={{1,2},{2,1},{5,6},{6,5},{9,10},{10,9},{13,14},{14,13},{17,18},{18,... | collective-permute-start | bytes 1572872 | tf_op jit(solution)/shard_map/ppermute | solution.py:380
  65.3 2.2 %shard_map.83 = (bf16[512,512]{1,0:T(8,128)(2,1)}, f32[8,128]{1,0:T(8,128)}) custom-call(bf16[1024,512]{1,0:T(8,128)(2,1)} %get-tuple-element.39.refs_0_, bf16[768,512]{1,0:T(8,128)(2,1)} %collective-permute-done.2.refs_1_, bf16[768,512]{1,0:T(8,128)(2,1)} %collective-permute-done.8.refs_2_.refs_8_, ...), custom_call_target="tpu_custom_call", output_to_operand_aliasing={{1}: (3, {})} | custom-call | flops 1 | bytes 1 | tf_op jit(solution)/shard_map/pallas_call | solution.py:33
  67.5 7.8 %collective-permute-done.10.refs_2_ = bf16[128,512]{1,0:T(8,128)(2,1)} collective-permute-done((bf16[128,512]{1,0:T(8,128)(2,1)}, bf16[128,512]{1,0:T(8,128)(2,1)}, u32[]{:S(2)}, u32[]{:S(2)}) %collective-permute-start.10) | collective-permute-done | bytes 131104 | tf_op jit(solution)/shard_map/ppermute | solution.py:380
  77.2 5.4 %shard_map.85 = (bf16[1024,512]{1,0:T(8,128)(2,1)}, f32[512,512]{1,0:T(8,128)}, f32[8,128]{1,0:T(8,128)}) custom-call(f32[1024,512]{1,0:T(8,128)} %get-tuple-element.51.refs_0_, bf16[128,512]{1,0:T(8,128)(2,1)} %get-tuple-element.55.refs_1_, bf16[128,512]{1,0:T(8,128)(2,1)} %get-tuple-element.61.refs_2_, ...), custom_call_target="tpu_custom_call", output_to_operand_aliasing={{2}: (10, {})} | custom-call | flops 1 | bytes 1 | tf_op jit(solution)/shard_map/pallas_call | solution.py:33
  82.7 3.0 %collective-permute-done.14.refs_3_ = bf16[512,512]{1,0:T(8,128)(2,1)} collective-permute-done((bf16[512,512]{1,0:T(8,128)(2,1)}, bf16[512,512]{1,0:T(8,128)(2,1)}, u32[]{:S(2)}, u32[]{:S(2)}) %collective-permute-start.14) | collective-permute-done | bytes 524320 | tf_op jit(solution)/shard_map/ppermute | solution.py:380
  85.6 2.5 %shard_map.86 = (bf16[1024,512]{1,0:T(8,128)(2,1)}, f32[8,128]{1,0:T(8,128)}) custom-call(bf16[1024,512]{1,0:T(8,128)(2,1)} %get-tuple-element.65.refs_0_, f32[512,512]{1,0:T(8,128)} %get-tuple-element.66.refs_1_, bf16[512,512]{1,0:T(8,128)(2,1)} %collective-permute-done.13.refs_2_, ...), custom_call_target="tpu_custom_call", output_to_operand_aliasing={{0}: (0, {}), {1}: (4, {})} | custom-call | flops 1 | bytes 1 | tf_op jit(solution)/shard_map/pallas_call | solution.py:33
  (29 shorter events, 4.3 us)
Async XLA Ops:
  4.8 21.8 %collective-permute-start = (bf16[768,512]{1,0:T(8,128)(2,1)}, bf16[768,512]{1,0:T(8,128)(2,1)}, u32[]{:S(2)}, u32[]{:S(2)}) collective-permute-start(bf16[768,512]{1,0:T(8,128)(2,1)} %get-tuple-element.40.refs_0_), channel_id=1, source_target_pairs={{0,1},{1,0},{2,3},{3,2},{4,5},{5,4},{6,7},{7,6},{8,9},{9,8},{10,11... | collective-permute-start | bytes 2359304 | tf_op jit(solution)/shard_map/ppermute | solution.py:380
  7.9 13.7 %collective-permute-start.1 = (bf16[2048,128]{1,0:T(8,128)(2,1)}, bf16[2048,128]{1,0:T(8,128)(2,1)}, u32[]{:S(2)}, u32[]{:S(2)}) collective-permute-start(bf16[2048,128]{1,0:T(8,128)(2,1)} %refs_1_.6), channel_id=1, source_target_pairs={{0,8},{4,12},{8,0},{12,4},{1,9},{5,13},{9,1},{13,5},{2,10},{6,14},... | collective-permute-start | bytes 1572872 | tf_op jit(solution)/shard_map/ppermute | solution.py:387
  9.4 21.2 %copy-start.1 = (s32[8]{0:T(128)S(1)}, s32[8]{0:T(128)}, u32[]{:S(2)}) copy-start(s32[8]{0:T(128)} %param.12) | copy-start | bytes 100
  9.4 21.2 %copy-start.2 = (s32[8]{0:T(128)S(1)}, s32[8]{0:T(128)}, u32[]{:S(2)}) copy-start(s32[8]{0:T(128)} %param.13) | copy-start | bytes 100
  9.4 21.2 %copy-start = (s32[1024,1]{0,1:T(1,128)S(1)}, s32[1024,1]{0,1:T(1,128)}, u32[]{:S(2)}) copy-start(s32[1024,1]{0,1:T(1,128)} %param.11) | copy-start | bytes 12292
  19.7 23.7 %collective-permute-start.3 = (bf16[768,512]{1,0:T(8,128)(2,1)}, bf16[768,512]{1,0:T(8,128)(2,1)}, u32[]{:S(2)}, u32[]{:S(2)}) collective-permute-start(bf16[768,512]{1,0:T(8,128)(2,1)} %get-tuple-element.44.refs_0_), channel_id=1, source_target_pairs={{0,1},{1,0},{2,3},{3,2},{4,5},{5,4},{6,7},{7,6},{8,9},{9,8},{10,11... | collective-permute-start | bytes 2359304 | tf_op jit(solution)/shard_map/ppermute | solution.py:380
  20.2 11.5 %collective-permute-start.4 = (bf16[2048,128]{1,0:T(8,128)(2,1)}, bf16[2048,128]{1,0:T(8,128)(2,1)}, u32[]{:S(2)}, u32[]{:S(2)}) collective-permute-start(bf16[2048,128]{1,0:T(8,128)(2,1)} %refs_1_.6), channel_id=1, source_target_pairs={{0,4},{4,0},{8,12},{12,8},{1,5},{5,1},{9,13},{13,9},{2,6},{6,2},{1... | collective-permute-start | bytes 1572872 | tf_op jit(solution)/shard_map/ppermute | solution.py:387
  21.6 10.1 %collective-permute-start.5 = (bf16[2048,128]{1,0:T(8,128)(2,1)}, bf16[2048,128]{1,0:T(8,128)(2,1)}, u32[]{:S(2)}, u32[]{:S(2)}) collective-permute-start(bf16[2048,128]{1,0:T(8,128)(2,1)} %get-tuple-element.45.refs_3_), channel_id=1, source_target_pairs={{0,4},{4,0},{8,12},{12,8},{1,5},{5,1},{9,13},{13,9},{2,6},{6,2},{1... | collective-permute-start | bytes 1572872 | tf_op jit(solution)/shard_map/ppermute | solution.py:387
  29.0 18.4 %collective-permute-start.2 = (bf16[768,512]{1,0:T(8,128)(2,1)}, bf16[768,512]{1,0:T(8,128)(2,1)}, u32[]{:S(2)}, u32[]{:S(2)}) collective-permute-start(bf16[768,512]{1,0:T(8,128)(2,1)} %get-tuple-element.43), channel_id=1, source_target_pairs={{1,2},{2,1},{5,6},{6,5},{9,10},{10,9},{13,14},{14,13},{17,18},{18,... | collective-permute-start | bytes 2359304 | tf_op jit(solution)/shard_map/ppermute | solution.py:380
  38.1 22.8 %collective-permute-start.6 = (bf16[640,512]{1,0:T(8,128)(2,1)}, bf16[640,512]{1,0:T(8,128)(2,1)}, u32[]{:S(2)}, u32[]{:S(2)}) collective-permute-start(bf16[640,512]{1,0:T(8,128)(2,1)} %get-tuple-element.52.refs_0_), channel_id=1, source_target_pairs={{0,1},{1,0},{2,3},{3,2},{4,5},{5,4},{6,7},{7,6},{8,9},{9,8},{10,11... | collective-permute-start | bytes 1966088 | tf_op jit(solution)/shard_map/ppermute | solution.py:380
  45.9 19.4 %collective-permute-start.8 = (bf16[768,512]{1,0:T(8,128)(2,1)}, bf16[768,512]{1,0:T(8,128)(2,1)}, u32[]{:S(2)}, u32[]{:S(2)}) collective-permute-start(bf16[768,512]{1,0:T(8,128)(2,1)} %get-tuple-element.56), channel_id=1, source_target_pairs={{1,2},{2,1},{5,6},{6,5},{9,10},{10,9},{13,14},{14,13},{17,18},{18,... | collective-permute-start | bytes 2359304 | tf_op jit(solution)/shard_map/ppermute | solution.py:380
  49.6 25.6 %collective-permute-start.9 = (bf16[512,512]{1,0:T(8,128)(2,1)}, bf16[512,512]{1,0:T(8,128)(2,1)}, u32[]{:S(2)}, u32[]{:S(2)}) collective-permute-start(bf16[512,512]{1,0:T(8,128)(2,1)} %get-tuple-element.59), channel_id=1, source_target_pairs={{0,1},{1,0},{2,3},{3,2},{4,5},{5,4},{6,7},{7,6},{8,9},{9,8},{10,11... | collective-permute-start | bytes 1572872 | tf_op jit(solution)/shard_map/ppermute | solution.py:380
  53.7 7.2 %collective-permute-start.7 = (bf16[128,512]{1,0:T(8,128)(2,1)}, bf16[128,512]{1,0:T(8,128)(2,1)}, u32[]{:S(2)}, u32[]{:S(2)}) collective-permute-start(bf16[128,512]{1,0:T(8,128)(2,1)} %refs_3_.1), channel_id=1, source_target_pairs={{0,8},{4,12},{8,0},{12,4},{1,9},{5,13},{9,1},{13,5},{2,10},{6,14},... | collective-permute-start | bytes 393224 | tf_op jit(solution)/shard_map/ppermute | solution.py:387
  63.2 12.1 %collective-permute-start.10 = (bf16[128,512]{1,0:T(8,128)(2,1)}, bf16[128,512]{1,0:T(8,128)(2,1)}, u32[]{:S(2)}, u32[]{:S(2)}) collective-permute-start(bf16[128,512]{1,0:T(8,128)(2,1)} %get-tuple-element.55.refs_1_), channel_id=1, source_target_pairs={{0,2},{2,0},{1,3},{3,1},{4,6},{6,4},{5,7},{7,5},{8,10},{10,8},{9,1... | collective-permute-start | bytes 393224 | tf_op jit(solution)/shard_map/ppermute | solution.py:380
  63.8 18.8 %collective-permute-start.13 = (bf16[512,512]{1,0:T(8,128)(2,1)}, bf16[512,512]{1,0:T(8,128)(2,1)}, u32[]{:S(2)}, u32[]{:S(2)}) collective-permute-start(bf16[512,512]{1,0:T(8,128)(2,1)} %get-tuple-element.67), channel_id=1, source_target_pairs={{1,2},{2,1},{5,6},{6,5},{9,10},{10,9},{13,14},{14,13},{17,18},{18,... | collective-permute-start | bytes 1572872 | tf_op jit(solution)/shard_map/ppermute | solution.py:380
  75.2 10.4 %collective-permute-start.14 = (bf16[512,512]{1,0:T(8,128)(2,1)}, bf16[512,512]{1,0:T(8,128)(2,1)}, u32[]{:S(2)}, u32[]{:S(2)}) collective-permute-start(bf16[512,512]{1,0:T(8,128)(2,1)} %get-tuple-element.68), channel_id=1, source_target_pairs={{0,1},{1,0},{2,3},{3,2},{4,5},{5,4},{6,7},{7,6},{8,9},{9,8},{10,11... | collective-permute-start | bytes 1572872 | tf_op jit(solution)/shard_map/ppermute | solution.py:380
  75.3 1.7 %collective-permute-start.11 = (bf16[128,512]{1,0:T(8,128)(2,1)}, bf16[128,512]{1,0:T(8,128)(2,1)}, u32[]{:S(2)}, u32[]{:S(2)}) collective-permute-start(bf16[128,512]{1,0:T(8,128)(2,1)} %refs_3_.1), channel_id=1, source_target_pairs={{0,4},{4,0},{8,12},{12,8},{1,5},{5,1},{9,13},{13,9},{2,6},{6,2},{1... | collective-permute-start | bytes 393224 | tf_op jit(solution)/shard_map/ppermute | solution.py:387
  75.3 1.9 %collective-permute-start.12 = (bf16[128,512]{1,0:T(8,128)(2,1)}, bf16[128,512]{1,0:T(8,128)(2,1)}, u32[]{:S(2)}, u32[]{:S(2)}) collective-permute-start(bf16[128,512]{1,0:T(8,128)(2,1)} %get-tuple-element.62.refs_5_), channel_id=1, source_target_pairs={{0,4},{4,0},{8,12},{12,8},{1,5},{5,1},{9,13},{13,9},{2,6},{6,2},{1... | collective-permute-start | bytes 393224 | tf_op jit(solution)/shard_map/ppermute | solution.py:387

commit v4 on v3

--- a/solution.py
+++ b/solution.py
@@ -11,13 +11,15 @@
 BF16 = jnp.bfloat16
 LANES = 128
 PIECES = 4
+LOW_PIECES = 2
 ANY = pl.BlockSpec(memory_space=pl.ANY)
 VMEM = pl.BlockSpec(memory_space=pltpu.VMEM)
 PARAMS = pltpu.CompilerParams(vmem_limit_bytes=64 * 1024 * 1024 - 128 * 1024)
 COST = pl.CostEstimate(flops=1, bytes_accessed=1, transcendentals=0)
-
-
-def call(kernel, outs, in_specs, scratch, token, *args, out_specs, aliases=None):
+MORE = pl.CostEstimate(flops=1 << 32, bytes_accessed=1 << 20, transcendentals=0)
+
+
+def call(kernel, outs, in_specs, scratch, token, *args, out_specs, aliases=None, cost=COST):
     n_in, n_out = len(args), len(outs)
     aliases = dict(aliases or {})
     if token is not None:
@@ -38,7 +40,7 @@
         scratch_shapes=scratch,
         input_output_aliases=aliases,
         compiler_params=PARAMS,
-        cost_estimate=COST,
+        cost_estimate=cost,
     )(*args)
 
 
@@ -80,10 +82,11 @@
 
 def fetch(hidden, weight, lo, rows, phase, first_row, h_buf, w_buf, h_sem, w_sem):
     depth, cols = w_buf.shape
-    step = depth // PIECES
+    pieces = w_sem.shape[0]
+    step = depth // pieces
     first = pl.multiple_of(block_of(phase) * cols, cols)
     h_copies, w_copies = [], []
-    for k in range(PIECES):
+    for k in range(pieces):
         span = pl.ds(k * step, step)
         if h_sem is not None:
             pair = (hidden.at[pl.ds(lo, rows), span], h_buf.at[pl.ds(lo - first_row, rows), span])
@@ -95,9 +98,10 @@
 
 def product(h_buf, w_buf, lo, rows, copies):
     h_copies, w_copies = copies
-    step = w_buf.shape[0] // PIECES
+    pieces = len(copies[1])
+    step = w_buf.shape[0] // pieces
     total = None
-    for k in range(PIECES):
+    for k in range(pieces):
         if h_copies:
             h_copies[k].wait()
         if w_copies:
@@ -134,6 +138,7 @@
     last = max(job[1] + job[2] for job in jobs)
     most = max(job[2] for job in jobs)
     count = len(jobs)
+    pieces = PIECES * 2 if count == 1 else PIECES
     return call(
         functools.partial(products_kernel, jobs, len(heights)),
         [jax.ShapeDtypeStruct((rows, cols), BF16) for rows in heights],
@@ -142,8 +147,8 @@
             pltpu.VMEM((last - first, depth), BF16),
             pltpu.VMEM((count, depth, cols), BF16),
             pltpu.VMEM((count, most, cols), BF16),
-            pltpu.SemaphoreType.DMA((count, PIECES)),
-            pltpu.SemaphoreType.DMA((count, PIECES)),
+            pltpu.SemaphoreType.DMA((count, pieces)),
+            pltpu.SemaphoreType.DMA((count, pieces)),
             pltpu.SemaphoreType.DMA((count,)),
         ],
         token,
@@ -161,9 +166,11 @@
         at += out.shape[0]
 
 
-def add(token, a, b, heights=None):
+def add(token, a, b, heights=None, cost=COST):
     outs = [jax.ShapeDtypeStruct((rows, a.shape[1]), BF16) for rows in heights or (a.shape[0],)]
-    return call(add_kernel, outs, [VMEM, VMEM], [], token, a, b, out_specs=[VMEM] * len(outs))
+    return call(
+        add_kernel, outs, [VMEM, VMEM], [], token, a, b, out_specs=[VMEM] * len(outs), cost=cost
+    )
 
 
 def add_middle_kernel(lo, spans, p, *rest):
@@ -195,15 +202,15 @@
 
 def low_kernel(hidden, y0, y1, y2, y3, code, _, out, h_buf, w_buf, acc, low, h_sem, w_sem, o_sem):
     rows, depth = hidden.shape
-    step = depth // PIECES
+    step = depth // LOW_PIECES
     h_copies, w_copies = [], []
-    for k in range(PIECES):
+    for k in range(LOW_PIECES):
         span = pl.ds(k * step, step)
         h_copies += copy_in([(hidden.at[:, span], h_buf.at[:, span])], h_sem.at[pl.ds(k, 1)])
         for p, y in enumerate((y0, y1, y2, y3)):
             pair = (y.at[span], w_buf.at[span, pl.ds(p * LANES, LANES)])
             w_copies += copy_in([pair], w_sem.at[pl.ds(4 * k + p, 1)])
-    for k in range(PIECES):
+    for k in range(LOW_PIECES):
         h_copies[k].wait()
         for p in range(4):
             w_copies[4 * k + p].wait()
@@ -243,8 +250,8 @@
             pltpu.VMEM((depth, 4 * LANES), BF16),
             pltpu.VMEM((rows, 4 * LANES), F32),
             pltpu.VMEM((rows // 8, 4 * LANES), BF16),
-            pltpu.SemaphoreType.DMA((PIECES,)),
-            pltpu.SemaphoreType.DMA((4 * PIECES,)),
+            pltpu.SemaphoreType.DMA((LOW_PIECES,)),
+            pltpu.SemaphoreType.DMA((4 * LOW_PIECES,)),
             pltpu.SemaphoreType.DMA((1,)),
         ],
         token,
@@ -338,6 +345,7 @@
         b,
         m,
         out_specs=[VMEM] * 2,
+        cost=MORE,
     )
 
 
@@ -409,14 +417,13 @@
     b12 = send(v, middle)
     v, t = add_middle(t, p2, 0, (b1a,), [(0, half)])
     m3a = send(v, near)
-    own, t = own_product(t, hidden, weight)
     up2, t = relay(t, up2)
     ups = (up, up1, up2, swap(up2, 1))
-    v, low, t = add(t, p1l, a2l, [half, rows // 8])
+    v, low, t = add(t, p1l, a2l, [half, rows // 8], MORE)
     b2b = send(v, middle)
     e2 = send(low, two)
+    own, t = own_product(t, hidden, weight)
     m, t = add_middle(t, p2, half, (b1a, b12), [(half, cut - half), (0, after)])
-    m, m3a, e2, t = relay(t, m, m3a, e2)
     m3b = send(m, near)
     out, rest, t = up_sum(t, own, low, e2, ups, code, b12, m3a)
     return last_sum(t, out, rest, b2b, m3b)

time: 88.5 us -> 86.8 us (0.981)
  waiting for transfers between devices: 19.7 us -> 13 us
  starting transfers between devices: 20.5 us -> 25.7 us
    ppermute x9, waiting for transfers between devices: 17 us -> 9.84 us  [send(): return lax.ppermute(v, 'tensor', pairs)]
    ppermute x9, starting transfers between devices: 17 us -> 22.4 us  [send(): return lax.ppermute(v, 'tensor', pairs)]
    pallas_call x14 -> x13, Pallas kernels: 46.6 us -> 46.5 us  [call(): pl.pallas_call(body, out_shape=(*outs, jax.ShapeDtypeStruct((8, LANES), F...]
  transfers between devices with their start and end apart: 15 -> 15, of which waited for: 7 -> 6; matrix products, arithmetic and copies ran while one was open for 1% -> 1% of each run, Pallas kernels for 45% -> 46%
where the time goes in v4:
time: 86.8 us; the launch traced here: 86.5 us
  Pallas kernels  46.5 us (54%)
  starting transfers between devices  25.7 us (30%)
  waiting for transfers between devices  13 us (15%)
  local copies, waits for them, and re-layouts  1.05 us (1%)
    pallas_call x13, Pallas kernels, call(): pl.pallas_call(body, out_shape=(*outs, jax.ShapeDtypeStruct((8, LANES), F...  46.5 us
    ppermute x9, starting transfers between devices, send(): return lax.ppermute(v, 'tensor', pairs)  22.4 us
    ppermute x9, waiting for transfers between devices, send(): return lax.ppermute(v, 'tensor', pairs)  9.84 us
    ppermute x6, starting transfers between devices, swap(): return lax.ppermute(v, 'dp', [(i, i ^ bit) for i in range(4)])  3.31 us
    ppermute x6, waiting for transfers between devices, swap(): return lax.ppermute(v, 'dp', [(i, i ^ bit) for i in range(4)])  3.13 us
  transfers between devices with their start and end apart: 15, of which 6 were waited for; matrix products, arithmetic and copies ran while one was open for 1% of the time, Pallas kernels for 46%

profile of v4, /device:TPU:0, one launch (start us, length us, event | category | flops | bytes accessed | tf_op | source)
XLA Modules:
  0.0 86.5 jit_solution(3326387423414296591)
XLA Ops:
  0.0 4.5 %shard_map.73 = (bf16[768,512]{1,0:T(8,128)(2,1)}, f32[8,128]{1,0:T(8,128)}) custom-call(bf16[1024,2048]{1,0:T(8,128)(2,1)} %refs_0_.7, bf16[2048,2048]{1,0:T(8,128)(2,1)} %refs_1_.7), custom_call_target="tpu_custom_call" | custom-call | flops 1 | bytes 1 | tf_op jit(solution)/shard_map/pallas_call | solution.py:35
  4.5 3.1 %collective-permute-start.3 = (bf16[768,512]{1,0:T(8,128)(2,1)}, bf16[768,512]{1,0:T(8,128)(2,1)}, u32[]{:S(2)}, u32[]{:S(2)}) collective-permute-start(bf16[768,512]{1,0:T(8,128)(2,1)} %get-tuple-element.38.refs_0_), channel_id=1, source_target_pairs={{0,1},{1,0},{2,3},{3,2},{4,5},{5,4},{6,7},{7,6},{8,9},{9,8},{10,11... | collective-permute-start | bytes 2359304 | tf_op jit(solution)/shard_map/ppermute | solution.py:388
  7.6 1.5 %collective-permute-start.1 = (bf16[2048,128]{1,0:T(8,128)(2,1)}, bf16[2048,128]{1,0:T(8,128)(2,1)}, u32[]{:S(2)}, u32[]{:S(2)}) collective-permute-start(bf16[2048,128]{1,0:T(8,128)(2,1)} %refs_1_.6), channel_id=1, source_target_pairs={{0,8},{4,12},{8,0},{12,4},{1,9},{5,13},{9,1},{13,5},{2,10},{6,14},... | collective-permute-start | bytes 1572872 | tf_op jit(solution)/shard_map/ppermute | solution.py:395
  9.1 10.3 %shard_map.74 = (bf16[768,512]{1,0:T(8,128)(2,1)}, bf16[640,512]{1,0:T(8,128)(2,1)}, bf16[1024,512]{1,0:T(8,128)(2,1)}, f32[8,128]{1,0:T(8,128)}) custom-call(bf16[1024,2048]{1,0:T(8,128)(2,1)} %refs_0_.7, bf16[2048,2048]{1,0:T(8,128)(2,1)} %refs_1_.7, f32[8,128]{1,0:T(8,128)} %get-tuple-element.34.refs_2_), custom_call_target="tpu_custom_call", output_to_operand_aliasing={{3}: (2, {})} | custom-call | flops 1 | bytes 1 | tf_op jit(solution)/shard_map/pallas_call | solution.py:35
  19.5 1.9 %collective-permute-done.1.refs_0_ = bf16[2048,128]{1,0:T(8,128)(2,1)} collective-permute-done((bf16[2048,128]{1,0:T(8,128)(2,1)}, bf16[2048,128]{1,0:T(8,128)(2,1)}, u32[]{:S(2)}, u32[]{:S(2)}) %collective-permute-start.1) | collective-permute-done | bytes 524320 | tf_op jit(solution)/shard_map/ppermute | solution.py:395
  21.7 4.5 %collective-permute-done.3.refs_1_ = bf16[768,512]{1,0:T(8,128)(2,1)} collective-permute-done((bf16[768,512]{1,0:T(8,128)(2,1)}, bf16[768,512]{1,0:T(8,128)(2,1)}, u32[]{:S(2)}, u32[]{:S(2)}) %collective-permute-start.3) | collective-permute-done | bytes 786464 | tf_op jit(solution)/shard_map/ppermute | solution.py:388
  26.2 2.4 %shard_map.76 = (bf16[768,512]{1,0:T(8,128)(2,1)}, f32[8,128]{1,0:T(8,128)}) custom-call(bf16[768,512]{1,0:T(8,128)(2,1)} %get-tuple-element.38.refs_0_, bf16[768,512]{1,0:T(8,128)(2,1)} %collective-permute-done.3.refs_1_, f32[8,128]{1,0:T(8,128)} %get-tuple-element.39.refs_2_), custom_call_target="tpu_custom_call", output_to_operand_aliasing={{1}: (2, {})} | custom-call | flops 1 | bytes 1 | tf_op jit(solution)/shard_map/pallas_call | solution.py:35
  28.6 1.5 %collective-permute-start.6 = (bf16[768,512]{1,0:T(8,128)(2,1)}, bf16[768,512]{1,0:T(8,128)(2,1)}, u32[]{:S(2)}, u32[]{:S(2)}) collective-permute-start(bf16[768,512]{1,0:T(8,128)(2,1)} %get-tuple-element.43), channel_id=1, source_target_pairs={{1,2},{2,1},{5,6},{6,5},{9,10},{10,9},{13,14},{14,13},{17,18},{18,... | collective-permute-start | bytes 2359304 | tf_op jit(solution)/shard_map/ppermute | solution.py:388
  31.3 6.5 %shard_map.77 = (bf16[640,512]{1,0:T(8,128)(2,1)}, f32[8,128]{1,0:T(8,128)}) custom-call(bf16[1024,2048]{1,0:T(8,128)(2,1)} %refs_0_.7, bf16[2048,128]{1,0:T(8,128)(2,1)} %refs_1_.6, bf16[2048,128]{1,0:T(8,128)(2,1)} %collective-permute-done.refs_2_, bf16[2048,128]{1,0:T(8,128)(2,1)} %get-tuple-element.36.refs_3_, ...), custom_call_target="tpu_custom_call", output_to_operand_aliasing={{0}: (6, {}), {1}: (7, {})} | custom-call | flops 1 | bytes 1 | tf_op jit(solution)/shard_map/pallas_call | solution.py:35
  37.8 3.9 %collective-permute-start.4 = (bf16[640,512]{1,0:T(8,128)(2,1)}, bf16[640,512]{1,0:T(8,128)(2,1)}, u32[]{:S(2)}, u32[]{:S(2)}) collective-permute-start(bf16[640,512]{1,0:T(8,128)(2,1)} %get-tuple-element.41.refs_0_), channel_id=1, source_target_pairs={{0,1},{1,0},{2,3},{3,2},{4,5},{5,4},{6,7},{7,6},{8,9},{9,8},{10,11... | collective-permute-start | bytes 1966088 | tf_op jit(solution)/shard_map/ppermute | solution.py:388
  43.0 2.4 %shard_map.78 = (bf16[768,512]{1,0:T(8,128)(2,1)}, f32[8,128]{1,0:T(8,128)}) custom-call(bf16[768,512]{1,0:T(8,128)(2,1)} %get-tuple-element.44.refs_0_, bf16[768,512]{1,0:T(8,128)(2,1)} %collective-permute-done.7.refs_1_, f32[8,128]{1,0:T(8,128)} %get-tuple-element.45.refs_2_), custom_call_target="tpu_custom_call", output_to_operand_aliasing={{1}: (2, {})} | custom-call | flops 1 | bytes 1 | tf_op jit(solution)/shard_map/pallas_call | solution.py:35
  45.5 1.5 %collective-permute-start.11 = (bf16[768,512]{1,0:T(8,128)(2,1)}, bf16[768,512]{1,0:T(8,128)(2,1)}, u32[]{:S(2)}, u32[]{:S(2)}) collective-permute-start(bf16[768,512]{1,0:T(8,128)(2,1)} %get-tuple-element.53), channel_id=1, source_target_pairs={{1,2},{2,1},{5,6},{6,5},{9,10},{10,9},{13,14},{14,13},{17,18},{18,... | collective-permute-start | bytes 2359304 | tf_op jit(solution)/shard_map/ppermute | solution.py:388
  47.0 1.8 %collective-permute-start.5 = (bf16[128,512]{1,0:T(8,128)(2,1)}, bf16[128,512]{1,0:T(8,128)(2,1)}, u32[]{:S(2)}, u32[]{:S(2)}) collective-permute-start(bf16[128,512]{1,0:T(8,128)(2,1)} %refs_3_.1), channel_id=1, source_target_pairs={{0,8},{4,12},{8,0},{12,4},{1,9},{5,13},{9,1},{13,5},{2,10},{6,14},... | collective-permute-start | bytes 393224 | tf_op jit(solution)/shard_map/ppermute | solution.py:395
  48.8 2.2 %shard_map.79 = (bf16[512,512]{1,0:T(8,128)(2,1)}, f32[8,128]{1,0:T(8,128)}) custom-call(bf16[1024,512]{1,0:T(8,128)(2,1)} %get-tuple-element.42.refs_0_, bf16[768,512]{1,0:T(8,128)(2,1)} %collective-permute-done.6.refs_1_, f32[8,128]{1,0:T(8,128)} %get-tuple-element.46.refs_2_), custom_call_target="tpu_custom_call", output_to_operand_aliasing={{1}: (2, {})} | custom-call | flops 1 | bytes 1 | tf_op jit(solution)/shard_map/pallas_call | solution.py:35
  52.3 3.9 %collective-permute-start.12 = (bf16[512,512]{1,0:T(8,128)(2,1)}, bf16[512,512]{1,0:T(8,128)(2,1)}, u32[]{:S(2)}, u32[]{:S(2)}) collective-permute-start(bf16[512,512]{1,0:T(8,128)(2,1)} %get-tuple-element.54), channel_id=1, source_target_pairs={{0,1},{1,0},{2,3},{3,2},{4,5},{5,4},{6,7},{7,6},{8,9},{9,8},{10,11... | collective-permute-start | bytes 1572872 | tf_op jit(solution)/shard_map/ppermute | solution.py:388
  56.4 2.3 %shard_map.81 = (bf16[512,512]{1,0:T(8,128)(2,1)}, bf16[128,512]{1,0:T(8,128)(2,1)}, f32[8,128]{1,0:T(8,128)}) custom-call(bf16[640,512]{1,0:T(8,128)(2,1)} %get-tuple-element.41.refs_0_, bf16[640,512]{1,0:T(8,128)(2,1)} %collective-permute-done.4.refs_1_, f32[8,128]{1,0:T(8,128)} %get-tuple-element.48.refs_2_), custom_call_target="tpu_custom_call", output_to_operand_aliasing={{2}: (2, {})} | custom-call | flops 4294967296 | bytes 1048576 | tf_op jit(solution)/shard_map/pallas_call | solution.py:35
  58.6 2.8 %collective-permute-start.8 = (bf16[128,512]{1,0:T(8,128)(2,1)}, bf16[128,512]{1,0:T(8,128)(2,1)}, u32[]{:S(2)}, u32[]{:S(2)}) collective-permute-start(bf16[128,512]{1,0:T(8,128)(2,1)} %get-tuple-element.51.refs_1_), channel_id=1, source_target_pairs={{0,2},{2,0},{1,3},{3,1},{4,6},{6,4},{5,7},{7,5},{8,10},{10,8},{9,1... | collective-permute-start | bytes 393224 | tf_op jit(solution)/shard_map/ppermute | solution.py:388
  61.4 5.7 %shard_map.82 = (f32[1024,512]{1,0:T(8,128)}, f32[8,128]{1,0:T(8,128)}) custom-call(bf16[1024,2048]{1,0:T(8,128)(2,1)} %refs_0_.7, bf16[2048,2048]{1,0:T(8,128)(2,1)} %refs_1_.7, f32[8,128]{1,0:T(8,128)} %get-tuple-element.49.refs_2_), custom_call_target="tpu_custom_call", output_to_operand_aliasing={{1}: (2, {})} | custom-call | flops 1 | bytes 1 | tf_op jit(solution)/shard_map/pallas_call | solution.py:35
  67.1 1.5 %collective-permute-start.13 = (bf16[512,512]{1,0:T(8,128)(2,1)}, bf16[512,512]{1,0:T(8,128)(2,1)}, u32[]{:S(2)}, u32[]{:S(2)}) collective-permute-start(bf16[512,512]{1,0:T(8,128)(2,1)} %get-tuple-element.59), channel_id=1, source_target_pairs={{1,2},{2,1},{5,6},{6,5},{9,10},{10,9},{13,14},{14,13},{17,18},{18,... | collective-permute-start | bytes 1572872 | tf_op jit(solution)/shard_map/ppermute | solution.py:388
  68.6 2.2 %shard_map.83 = (bf16[512,512]{1,0:T(8,128)(2,1)}, f32[8,128]{1,0:T(8,128)}) custom-call(bf16[1024,512]{1,0:T(8,128)(2,1)} %get-tuple-element.42.refs_0_, bf16[768,512]{1,0:T(8,128)(2,1)} %collective-permute-done.6.refs_1_, bf16[768,512]{1,0:T(8,128)(2,1)} %collective-permute-done.11.refs_2_.refs_8_, ...), custom_call_target="tpu_custom_call", output_to_operand_aliasing={{1}: (3, {})} | custom-call | flops 1 | bytes 1 | tf_op jit(solution)/shard_map/pallas_call | solution.py:35
  70.8 3.8 %collective-permute-start.14 = (bf16[512,512]{1,0:T(8,128)(2,1)}, bf16[512,512]{1,0:T(8,128)(2,1)}, u32[]{:S(2)}, u32[]{:S(2)}) collective-permute-start(bf16[512,512]{1,0:T(8,128)(2,1)} %get-tuple-element.60), channel_id=1, source_target_pairs={{0,1},{1,0},{2,3},{3,2},{4,5},{5,4},{6,7},{7,6},{8,9},{9,8},{10,11... | collective-permute-start | bytes 1572872 | tf_op jit(solution)/shard_map/ppermute | solution.py:388
  74.6 5.5 %shard_map.84 = (bf16[1024,512]{1,0:T(8,128)(2,1)}, f32[512,512]{1,0:T(8,128)}, f32[8,128]{1,0:T(8,128)}) custom-call(f32[1024,512]{1,0:T(8,128)} %get-tuple-element.50.refs_0_, bf16[128,512]{1,0:T(8,128)(2,1)} %get-tuple-element.51.refs_1_, bf16[128,512]{1,0:T(8,128)(2,1)} %collective-permute-done.8.refs_2_, ...), custom_call_target="tpu_custom_call", output_to_operand_aliasing={{2}: (10, {})} | custom-call | flops 4294967296 | bytes 1048576 | tf_op jit(solution)/shard_map/pallas_call | solution.py:35
  80.1 3.9 %collective-permute-done.14.refs_3_ = bf16[512,512]{1,0:T(8,128)(2,1)} collective-permute-done((bf16[512,512]{1,0:T(8,128)(2,1)}, bf16[512,512]{1,0:T(8,128)(2,1)}, u32[]{:S(2)}, u32[]{:S(2)}) %collective-permute-start.14) | collective-permute-done | bytes 524320 | tf_op jit(solution)/shard_map/ppermute | solution.py:388
  84.0 2.5 %shard_map.85 = (bf16[1024,512]{1,0:T(8,128)(2,1)}, f32[8,128]{1,0:T(8,128)}) custom-call(bf16[1024,512]{1,0:T(8,128)(2,1)} %get-tuple-element.57.refs_0_, f32[512,512]{1,0:T(8,128)} %get-tuple-element.58.refs_1_, bf16[512,512]{1,0:T(8,128)(2,1)} %collective-permute-done.13.refs_2_, ...), custom_call_target="tpu_custom_call", output_to_operand_aliasing={{0}: (0, {}), {1}: (4, {})} | custom-call | flops 1 | bytes 1 | tf_op jit(solution)/shard_map/pallas_call | solution.py:35
  (28 shorter events, 4.3 us)
Async XLA Ops:
  4.5 21.6 %collective-permute-start.3 = (bf16[768,512]{1,0:T(8,128)(2,1)}, bf16[768,512]{1,0:T(8,128)(2,1)}, u32[]{:S(2)}, u32[]{:S(2)}) collective-permute-start(bf16[768,512]{1,0:T(8,128)(2,1)} %get-tuple-element.38.refs_0_), channel_id=1, source_target_pairs={{0,1},{1,0},{2,3},{3,2},{4,5},{5,4},{6,7},{7,6},{8,9},{9,8},{10,11... | collective-permute-start | bytes 2359304 | tf_op jit(solution)/shard_map/ppermute | solution.py:388
  7.6 13.7 %collective-permute-start.1 = (bf16[2048,128]{1,0:T(8,128)(2,1)}, bf16[2048,128]{1,0:T(8,128)(2,1)}, u32[]{:S(2)}, u32[]{:S(2)}) collective-permute-start(bf16[2048,128]{1,0:T(8,128)(2,1)} %refs_1_.6), channel_id=1, source_target_pairs={{0,8},{4,12},{8,0},{12,4},{1,9},{5,13},{9,1},{13,5},{2,10},{6,14},... | collective-permute-start | bytes 1572872 | tf_op jit(solution)/shard_map/ppermute | solution.py:395
  9.1 22.2 %collective-permute-start = (bf16[2048,128]{1,0:T(8,128)(2,1)}, bf16[2048,128]{1,0:T(8,128)(2,1)}, u32[]{:S(2)}, u32[]{:S(2)}) collective-permute-start(bf16[2048,128]{1,0:T(8,128)(2,1)} %refs_1_.6), channel_id=1, source_target_pairs={{0,4},{4,0},{8,12},{12,8},{1,5},{5,1},{9,13},{13,9},{2,6},{6,2},{1... | collective-permute-start | bytes 1572872 | tf_op jit(solution)/shard_map/ppermute | solution.py:395
  9.1 21.0 %copy-start.1 = (s32[8]{0:T(128)S(1)}, s32[8]{0:T(128)}, u32[]{:S(2)}) copy-start(s32[8]{0:T(128)} %param.12) | copy-start | bytes 100
  9.1 21.0 %copy-start.2 = (s32[8]{0:T(128)S(1)}, s32[8]{0:T(128)}, u32[]{:S(2)}) copy-start(s32[8]{0:T(128)} %param.13) | copy-start | bytes 100
  9.1 21.0 %copy-start = (s32[1024,1]{0,1:T(1,128)S(1)}, s32[1024,1]{0,1:T(1,128)}, u32[]{:S(2)}) copy-start(s32[1024,1]{0,1:T(1,128)} %param.11) | copy-start | bytes 12292
  21.3 10.0 %collective-permute-start.2 = (bf16[2048,128]{1,0:T(8,128)(2,1)}, bf16[2048,128]{1,0:T(8,128)(2,1)}, u32[]{:S(2)}, u32[]{:S(2)}) collective-permute-start(bf16[2048,128]{1,0:T(8,128)(2,1)} %get-tuple-element.36.refs_3_), channel_id=1, source_target_pairs={{0,4},{4,0},{8,12},{12,8},{1,5},{5,1},{9,13},{13,9},{2,6},{6,2},{1... | collective-permute-start | bytes 1572872 | tf_op jit(solution)/shard_map/ppermute | solution.py:395
  21.3 21.7 %collective-permute-start.7 = (bf16[768,512]{1,0:T(8,128)(2,1)}, bf16[768,512]{1,0:T(8,128)(2,1)}, u32[]{:S(2)}, u32[]{:S(2)}) collective-permute-start(bf16[768,512]{1,0:T(8,128)(2,1)} %get-tuple-element.44.refs_0_), channel_id=1, source_target_pairs={{0,1},{1,0},{2,3},{3,2},{4,5},{5,4},{6,7},{7,6},{8,9},{9,8},{10,11... | collective-permute-start | bytes 2359304 | tf_op jit(solution)/shard_map/ppermute | solution.py:388
  28.6 20.2 %collective-permute-start.6 = (bf16[768,512]{1,0:T(8,128)(2,1)}, bf16[768,512]{1,0:T(8,128)(2,1)}, u32[]{:S(2)}, u32[]{:S(2)}) collective-permute-start(bf16[768,512]{1,0:T(8,128)(2,1)} %get-tuple-element.43), channel_id=1, source_target_pairs={{1,2},{2,1},{5,6},{6,5},{9,10},{10,9},{13,14},{14,13},{17,18},{18,... | collective-permute-start | bytes 2359304 | tf_op jit(solution)/shard_map/ppermute | solution.py:388
  37.8 18.6 %collective-permute-start.4 = (bf16[640,512]{1,0:T(8,128)(2,1)}, bf16[640,512]{1,0:T(8,128)(2,1)}, u32[]{:S(2)}, u32[]{:S(2)}) collective-permute-start(bf16[640,512]{1,0:T(8,128)(2,1)} %get-tuple-element.41.refs_0_), channel_id=1, source_target_pairs={{0,1},{1,0},{2,3},{3,2},{4,5},{5,4},{6,7},{7,6},{8,9},{9,8},{10,11... | collective-permute-start | bytes 1966088 | tf_op jit(solution)/shard_map/ppermute | solution.py:388
  45.5 21.6 %collective-permute-start.11 = (bf16[768,512]{1,0:T(8,128)(2,1)}, bf16[768,512]{1,0:T(8,128)(2,1)}, u32[]{:S(2)}, u32[]{:S(2)}) collective-permute-start(bf16[768,512]{1,0:T(8,128)(2,1)} %get-tuple-element.53), channel_id=1, source_target_pairs={{1,2},{2,1},{5,6},{6,5},{9,10},{10,9},{13,14},{14,13},{17,18},{18,... | collective-permute-start | bytes 2359304 | tf_op jit(solution)/shard_map/ppermute | solution.py:388
  47.0 5.3 %collective-permute-start.5 = (bf16[128,512]{1,0:T(8,128)(2,1)}, bf16[128,512]{1,0:T(8,128)(2,1)}, u32[]{:S(2)}, u32[]{:S(2)}) collective-permute-start(bf16[128,512]{1,0:T(8,128)(2,1)} %refs_3_.1), channel_id=1, source_target_pairs={{0,8},{4,12},{8,0},{12,4},{1,9},{5,13},{9,1},{13,5},{2,10},{6,14},... | collective-permute-start | bytes 393224 | tf_op jit(solution)/shard_map/ppermute | solution.py:395
  48.8 21.9 %collective-permute-start.9 = (bf16[128,512]{1,0:T(8,128)(2,1)}, bf16[128,512]{1,0:T(8,128)(2,1)}, u32[]{:S(2)}, u32[]{:S(2)}) collective-permute-start(bf16[128,512]{1,0:T(8,128)(2,1)} %refs_3_.1), channel_id=1, source_target_pairs={{0,4},{4,0},{8,12},{12,8},{1,5},{5,1},{9,13},{13,9},{2,6},{6,2},{1... | collective-permute-start | bytes 393224 | tf_op jit(solution)/shard_map/ppermute | solution.py:395
  52.3 22.3 %collective-permute-start.10 = (bf16[128,512]{1,0:T(8,128)(2,1)}, bf16[128,512]{1,0:T(8,128)(2,1)}, u32[]{:S(2)}, u32[]{:S(2)}) collective-permute-start(bf16[128,512]{1,0:T(8,128)(2,1)} %get-tuple-element.52.refs_5_), channel_id=1, source_target_pairs={{0,4},{4,0},{8,12},{12,8},{1,5},{5,1},{9,13},{13,9},{2,6},{6,2},{1... | collective-permute-start | bytes 393224 | tf_op jit(solution)/shard_map/ppermute | solution.py:395
  52.3 22.3 %collective-permute-start.12 = (bf16[512,512]{1,0:T(8,128)(2,1)}, bf16[512,512]{1,0:T(8,128)(2,1)}, u32[]{:S(2)}, u32[]{:S(2)}) collective-permute-start(bf16[512,512]{1,0:T(8,128)(2,1)} %get-tuple-element.54), channel_id=1, source_target_pairs={{0,1},{1,0},{2,3},{3,2},{4,5},{5,4},{6,7},{7,6},{8,9},{9,8},{10,11... | collective-permute-start | bytes 1572872 | tf_op jit(solution)/shard_map/ppermute | solution.py:388
  58.6 15.9 %collective-permute-start.8 = (bf16[128,512]{1,0:T(8,128)(2,1)}, bf16[128,512]{1,0:T(8,128)(2,1)}, u32[]{:S(2)}, u32[]{:S(2)}) collective-permute-start(bf16[128,512]{1,0:T(8,128)(2,1)} %get-tuple-element.51.refs_1_), channel_id=1, source_target_pairs={{0,2},{2,0},{1,3},{3,1},{4,6},{6,4},{5,7},{7,5},{8,10},{10,8},{9,1... | collective-permute-start | bytes 393224 | tf_op jit(solution)/shard_map/ppermute | solution.py:388
  67.1 13.0 %collective-permute-start.13 = (bf16[512,512]{1,0:T(8,128)(2,1)}, bf16[512,512]{1,0:T(8,128)(2,1)}, u32[]{:S(2)}, u32[]{:S(2)}) collective-permute-start(bf16[512,512]{1,0:T(8,128)(2,1)} %get-tuple-element.59), channel_id=1, source_target_pairs={{1,2},{2,1},{5,6},{6,5},{9,10},{10,9},{13,14},{14,13},{17,18},{18,... | collective-permute-start | bytes 1572872 | tf_op jit(solution)/shard_map/ppermute | solution.py:388
  70.8 13.2 %collective-permute-start.14 = (bf16[512,512]{1,0:T(8,128)(2,1)}, bf16[512,512]{1,0:T(8,128)(2,1)}, u32[]{:S(2)}, u32[]{:S(2)}) collective-permute-start(bf16[512,512]{1,0:T(8,128)(2,1)} %get-tuple-element.60), channel_id=1, source_target_pairs={{0,1},{1,0},{2,3},{3,2},{4,5},{5,4},{6,7},{7,6},{8,9},{9,8},{10,11... | collective-permute-start | bytes 1572872 | tf_op jit(solution)/shard_map/ppermute | solution.py:388
